TPU v7x, 256 devices: a whole 4x4x8 slice. The times are simulated.
256 devices in a mesh: ens: 4 (over z_lo, core), tile: 64 (over y, x, z_hi).
Axes of the slice: x: 4, y: 4, z: 8 (z_hi: 4, z_lo: 2; z = z_hi * 2 + z_lo), core: 2. Of those that a mesh axis runs over, the one named last changes fastest.
Arguments:
- inputs: bfloat16 [8, 12, 1024, 384], P('ens', None, 'tile'), may hold values from -6 to 6
- target: float32 [77, 12, 1024], P(None, None, 'tile'), may hold values from -6 to 6
- land_sea: int32 [12, 1024], P(None, 'tile'), may hold values from 0 to 1, as said below
- kernel: float32 [7, 7, 384], replicated, may hold values from -0.875 to 0.875
- norm_gain: float32 [384], replicated, may hold values from 0.5 to 1.5
- w_expand: bfloat16 [384, 1536], replicated, may hold values from -0.3125 to 0.3125
- w_reduce: bfloat16 [1536, 384], replicated, may hold values from -0.15625 to 0.15625
- head_weight: bfloat16 [384, 77], replicated, may hold values from -0.3125 to 0.3125
Outputs:
- grad_inputs: float32 [8, 12, 1024, 384], P('ens', None, 'tile')
- grad_kernel: float32 [7, 7, 384], replicated
- grad_gain: float32 [384], replicated
- grad_expand: float32 [384, 1536], replicated
- grad_reduce: float32 [1536, 384], replicated
- grad_head: float32 [384, 77], replicated
Inputs may be any that keep to these rules, and one draw needn't show every extreme that they name: `land_sea`: number the tiles of 16 longitude cells k = 0 to 63 from west to east. Tile k holds between min(48 + 96 * k // 63, 144) and that bound plus 192 // 8 - 1 ocean cells, never more than 144; the easternmost tile holds exactly 144.
All inputs are finite; a program needn't handle non-finite values.
Results may differ from a plain program's by a relative error of at most 0.011.
Values may be sent and summed in bfloat16 or wider, within the bound.
A program may use at most 64 MiB of HBM per device.

v0:
```python
import jax
import jax.numpy as jnp
from jax import lax
from jax.sharding import PartitionSpec as P

FAIR_WEIGHT = 0.95
SMOOTHING = 0.5
NORM_EPS = 1e-06


def padded(cells, sides, width):
    for axis, dim in sides:
        count = lax.axis_size(axis)
        head = lax.slice_in_dim(cells, 0, width, axis=dim)
        tail = lax.slice_in_dim(cells, cells.shape[dim] - width, cells.shape[dim], axis=dim)
        cells = jnp.concatenate(
            [
                lax.ppermute(tail, axis, [(i, (i + 1) % count) for i in range(count)]),
                cells,
                lax.ppermute(head, axis, [((i + 1) % count, i) for i in range(count)]),
            ],
            axis=dim,
        )
    return cells


def local_gradient(offset):
    return offset / jnp.sqrt(offset * offset + SMOOTHING * SMOOTHING)


def spread_rows(extended, kernel, height, breadth):
    extent = kernel.shape[0]
    margin = extent // 2
    padded_field = jnp.pad(extended, ((0, 0), (margin, margin), (0, 0), (0, 0)))
    result = jnp.zeros((extended.shape[0], height, breadth, extended.shape[3]), jnp.float32)
    for lat_step in range(extent):
        for lon_step in range(extent):
            result = (
                result
                + padded_field[:, lat_step : lat_step + height, lon_step : lon_step + breadth]
                * kernel[lat_step, lon_step]
            )
    return (result, padded_field)


def score_gradient(prediction, observed_rows, water_rows):
    pooled_members = lax.all_gather(prediction, "ens", axis=1, tiled=True)
    ensemble_members = pooled_members.shape[1]
    ensemble_spread = jnp.sum(
        local_gradient(prediction[:, :, None, :] - pooled_members[:, None, :, :]), axis=2
    )
    self_term = local_gradient(prediction - observed_rows[:, None, :]) / ensemble_members
    return (
        self_term - FAIR_WEIGHT / (ensemble_members * (ensemble_members - 1)) * ensemble_spread
    ) * water_rows[None, None, :]


def block_rows(
    mixed_rows, input_rows, observed_rows, water_rows, norm_gain, w_expand, w_reduce, head_weight
):
    ensemble_count, row_counts, channels = mixed_rows.shape
    output_fields = head_weight.shape[1]
    centre = mixed_rows - jnp.mean(mixed_rows, axis=-1, keepdims=True)
    reciprocal = lax.rsqrt(jnp.mean(centre * centre, axis=-1, keepdims=True) + NORM_EPS)
    standard_deviation = centre * reciprocal
    normalized = (standard_deviation * norm_gain).astype(jnp.bfloat16).reshape(-1, channels)
    prior_field = jnp.dot(normalized, w_expand, preferred_element_type=jnp.float32)
    hidden_state = jax.nn.gelu(prior_field).astype(jnp.bfloat16)
    summed = input_rows.reshape(-1, channels) + jnp.dot(
        hidden_state, w_reduce, preferred_element_type=jnp.float32
    )
    block_result = summed.astype(jnp.bfloat16)
    prediction = lax.dot_general(
        head_weight, block_result, (((0,), (1,)), ((), ())), preferred_element_type=jnp.float32
    )
    prediction = prediction.reshape(output_fields, ensemble_count, row_counts)
    local_gradients = score_gradient(prediction, observed_rows, water_rows)
    slopes_b = local_gradients.astype(jnp.bfloat16).reshape(output_fields, -1)
    g_head = lax.dot_general(
        block_result, slopes_b, (((0,), (1,)), ((), ())), preferred_element_type=jnp.float32
    )
    d_block = lax.dot_general(
        slopes_b, head_weight, (((0,), (1,)), ((), ())), preferred_element_type=jnp.float32
    )
    d_block_b = d_block.astype(jnp.bfloat16)
    g_reduce = lax.dot_general(
        hidden_state, d_block_b, (((0,), (0,)), ((), ())), preferred_element_type=jnp.float32
    )
    d_hidden = lax.dot_general(
        d_block_b, w_reduce, (((1,), (1,)), ((), ())), preferred_element_type=jnp.float32
    )
    _, pullback = jax.vjp(jax.nn.gelu, prior_field)
    d_before = pullback(d_hidden)[0].astype(jnp.bfloat16)
    g_expand = lax.dot_general(
        normalized, d_before, (((0,), (0,)), ((), ())), preferred_element_type=jnp.float32
    )
    d_normed = lax.dot_general(
        d_before, w_expand, (((1,), (1,)), ((), ())), preferred_element_type=jnp.float32
    )
    d_normed = d_normed.reshape(ensemble_count, row_counts, channels)
    g_gain = jnp.sum(d_normed * standard_deviation, axis=(0, 1))
    scaled = d_normed * norm_gain
    d_mixed = reciprocal * (
        scaled
        - jnp.mean(scaled, axis=-1, keepdims=True)
        - standard_deviation * jnp.mean(scaled * standard_deviation, axis=-1, keepdims=True)
    )
    d_direct = d_block.reshape(ensemble_count, row_counts, channels)
    return (d_mixed, d_direct, (g_expand, g_reduce, g_head, g_gain))


def on_device(inputs, target, land_sea, kernel, norm_gain, w_expand, w_reduce, head_weight):
    ensemble_count, height, breadth, channels = inputs.shape
    output_fields = target.shape[0]
    extent = kernel.shape[0]
    margin = extent // 2
    cell_count = height * breadth
    rim_inputs = padded(inputs, (("tile", 2),), margin)
    mixed_field, padded_field = spread_rows(rim_inputs, kernel, height, breadth)
    mixed_flat = mixed_field.reshape(ensemble_count, cell_count, channels)
    input_flat = inputs.reshape(ensemble_count, cell_count, channels)
    truth_flat = target.reshape(output_fields, cell_count)
    ocean_flat = land_sea.reshape(cell_count).astype(jnp.float32)
    d_mixed, d_direct, weight_terms = block_rows(
        mixed_flat, input_flat, truth_flat, ocean_flat, norm_gain, w_expand, w_reduce, head_weight
    )
    d_mixed = d_mixed.reshape(ensemble_count, height, breadth, channels)
    rim_grad = padded(d_mixed.astype(jnp.bfloat16), (("tile", 2),), margin).astype(d_mixed.dtype)
    backward_field, _ = spread_rows(rim_grad, kernel[::-1, ::-1], height, breadth)
    grad_inputs = d_direct.reshape(ensemble_count, height, breadth, channels) + backward_field
    g_kernel = jnp.stack(
        [
            jnp.stack(
                [
                    jnp.sum(
                        d_mixed
                        * padded_field[
                            :, lat_step : lat_step + height, lon_step : lon_step + breadth
                        ],
                        axis=(0, 1, 2),
                    )
                    for lon_step in range(extent)
                ]
            )
            for lat_step in range(extent)
        ]
    )
    ocean_total = jnp.sum(ocean_flat)
    g_expand, g_reduce, g_head, g_gain = weight_terms
    g_expand, g_reduce, g_head, g_kernel, g_gain, ocean_total = lax.psum(
        (g_expand, g_reduce, g_head, g_kernel, g_gain, ocean_total), ("ens", "tile")
    )
    ocean_total = ocean_total / lax.axis_size("ens")
    return (
        grad_inputs,
        g_kernel / ocean_total,
        g_gain / ocean_total,
        g_expand / ocean_total,
        g_reduce / ocean_total,
        g_head / ocean_total,
    )


def solution(mesh):
    return jax.shard_map(
        on_device,
        mesh=mesh,
        in_specs=(
            P("ens", None, "tile", None),
            P(None, None, "tile"),
            P(None, "tile"),
            P(),
            P(),
            P(),
            P(),
            P(),
        ),
        out_specs=(P("ens", None, "tile", None), P(), P(), P(), P(), P()),
        check_vma=False,
    )
```

profile of v0, /device:TPU:1, one launch (start us, length us, event | category | flops | bytes accessed | tf_op | source)
XLA Modules:
  0.0 365.1 jit_solution(6427193147626626731)
XLA Ops:
  7.2 1.2 fusion.216
  8.4 11.6 %collective-permute-start.1 = (bf16[2,12,3,384]{3,2,1,0:T(4,128)(2,1)S(1)}, bf16[2,12,3,384]{3,2,1,0:T(4,128)(2,1)S(1)}, u32[]{:S(2)}, u32[]{:S(2)}) collective-permute-start(bf16[2,12,3,384]{3,2,1,0:T(4,128)(2,1)S(1)} %get-tuple-element.130), channel_id=1, source_target_pairs={{1,0},{2,1},{3,2},{4,3},{5,4},{6,5},{7,6},{8,7},{9,8},{10,9},{11,1... | collective-permute-start | bytes 165896 | tf_op jit(solution)/shard_map/ppermute | solution.py:20
  20.0 1.8 slice_reduce_fusion.48
  21.9 1.9 slice_reduce_fusion.47
  23.8 1.0 constant_dynamic-update-slice_fusion.1
  24.8 1.6 slice_reduce_fusion.46
  26.4 1.0 copy.18
  29.8 1.2 fusion.16
  31.0 5.6 %fusion.213 = (f32[2,12,16]{2,1,0:T(8,128)S(1)}, f32[2,12,16,384]{3,2,1,0:T(8,128)S(1)}) fusion(f32[384]{0:T(512)} %get-tuple-element.115, bf16[2,18,22,384]{3,2,1,0:T(8,128)(2,1)S(1)} %fusion.16, f32[384]{0:T(512)} %get-tuple-element.116, f32[384]{0:T(512)S(1)} %get-tuple-element.69, f32[384]{0:T(512)S(1)} %get-tuple-element.70, ...), kind=kLoop, calls=%fused_computation.449 | loop fusion | flops 23002752 | bytes 14287872 | tf_op jit(solution)/shard_map/reduce_sum | solution.py:63
  39.0 1.0 multiply_convert_fusion.1
  40.8 1.0 fusion.11
  42.9 0.9 convolution_bitcast_fusion
  43.8 1.7 sub.73
  45.5 1.0 copy.19
  46.5 10.2 %all_gather.3 = f32[77,8,192]{2,0,1:T(8,128)S(1)} all-gather(f32[77,2,192]{2,0,1:T(8,128)S(1)} %copy.19), channel_id=1, replica_groups=mesh['ens'=4,'tile'=64] {'ens'}, dimensions={1}, use_global_device_ids=true | all-gather | bytes 591360 | tf_op jit(solution)/shard_map/all_gather | solution.py:47
  58.5 1.7 mul.1234
  60.3 1.1 multiply_convert_fusion.2
  61.3 1.1 fusion.218
  62.5 4.2 %fusion.6 = bf16[384,1536]{1,0:T(8,128)(2,1)S(1)} fusion(f32[384,1536]{1,0:T(8,128)} %copy-done.5, bf16[1536,384]{1,0:T(8,128)(2,1)} %param.14, f32[384,384]{1,0:T(8,128)S(1)} %fusion.218), kind=kOutput, calls=%fused_computation.50 | convolution fusion | flops 464928768 | bytes 5308416 | tf_op jit(solution)/shard_map/dot_general | solution.py:89
  66.7 2.2 multiply_reduce_fusion
  68.9 2.2 fusion.219
  71.1 2.6 fusion.207
  74.6 3.4 fusion.112
  78.1 1.6 fusion.94
  79.8 1.2 fusion.91
  83.4 6.3 %collective-permute-start.3 = (bf16[2,12,3,384]{3,2,1,0:T(4,128)(2,1)S(1)}, bf16[2,12,3,384]{3,2,1,0:T(4,128)(2,1)S(1)}, u32[]{:S(2)}, u32[]{:S(2)}) collective-permute-start(bf16[2,12,3,384]{3,2,1,0:T(4,128)(2,1)S(1)} %get-tuple-element.128), channel_id=1, source_target_pairs={{1,0},{2,1},{3,2},{4,3},{5,4},{6,5},{7,6},{8,7},{9,8},{10,9},{11,1... | collective-permute-start | bytes 165896 | tf_op jit(solution)/shard_map/ppermute | solution.py:20
  89.7 79.2 %all-reduce.2 = (f32[]{:T(128)}, f32[384]{0:T(512)S(1)}) all-reduce(f32[]{:T(128)} %convert_reduce_fusion, f32[384]{0:T(512)} %get-tuple-element.48), channel_id=1, replica_groups=mesh['ens'=4,'tile'=64] {'ens','tile'}, use_global_device_ids=true, to_apply=%region_56.57 | all-reduce | flops 385 | bytes 3080 | tf_op jit(solution)/shard_map/psum | solution.py:150
  170.7 5.3 %fusion.178 = f32[2,12,16,384]{3,2,1,0:T(8,128)} fusion(f32[2,12,16,384]{3,2,1,0:T(8,128)S(1)} %bitcast.46, f32[2,12,22,384]{3,2,1,0:T(8,128)S(1)} %maximum_convert_fusion, f32[384]{0:T(512)} %get-tuple-element.115, f32[384]{0:T(512)} %get-tuple-element.116, f32[384]{0:T(512)S(1)} %copy-done.18, f32[384]{0:T(512)S(1)} %copy-done.20, f32[384]{0:T(512)S(1)} %copy-done.22, ...), kind=kLoop, calls=%fused_computation.327 | loop fusion | flops 14450688 | bytes 6287872 | tf_op jit(solution)/shard_map/add | solution.py:130
  176.0 175.0 %all-reduce.6.cloned.1.call-done = (f32[7,7,384]{2,1,0:T(8,128)}, f32[384,1536]{1,0:T(8,128)}, f32[1536,384]{1,0:T(8,128)}, f32[384,77]{0,1:T(8,128)}) async-done(((f32[7,7,384]{2,1,0:T(8,128)}, f32[384,1536]{1,0:T(8,128)}, f32[1536,384]{1,0:T(8,128)}, f32[384,77]{0,1:T(8,128)}), (f32[7,7,384]{2,1,0:T(8,128)}, f32[384,1536]{1,0:T(8,128)}, f32[1536,384]{1,0:T(8,128)}, ...) | async-done | bytes 4912144 | tf_op jit(solution)/shard_map/psum | solution.py:150
  351.0 1.5 broadcast_divide_fusion.3
  352.6 3.4 broadcast_divide_fusion.1
  356.0 1.6 broadcast_divide_fusion
  (280 shorter events, 12.4 us)
Async XLA Ops:
  7.2 343.8 %all-reduce.6.cloned.1.call-start = ((), (), s32[]{:S(2)}) async-start(), calls=%async_computation | async-start | bytes 9854976 | tf_op jit(solution)/shard_map/psum | solution.py:150
  8.4 21.3 %collective-permute-start.1 = (bf16[2,12,3,384]{3,2,1,0:T(4,128)(2,1)S(1)}, bf16[2,12,3,384]{3,2,1,0:T(4,128)(2,1)S(1)}, u32[]{:S(2)}, u32[]{:S(2)}) collective-permute-start(bf16[2,12,3,384]{3,2,1,0:T(4,128)(2,1)S(1)} %get-tuple-element.130), channel_id=1, source_target_pairs={{1,0},{2,1},{3,2},{4,3},{5,4},{6,5},{7,6},{8,7},{9,8},{10,9},{11,1... | collective-permute-start | bytes 165896 | tf_op jit(solution)/shard_map/ppermute | solution.py:20
  20.0 9.8 %collective-permute-start = (bf16[2,12,3,384]{3,2,1,0:T(4,128)(2,1)S(1)}, bf16[2,12,3,384]{3,2,1,0:T(4,128)(2,1)S(1)}, u32[]{:S(2)}, u32[]{:S(2)}) collective-permute-start(bf16[2,12,3,384]{3,2,1,0:T(4,128)(2,1)S(1)} %get-tuple-element.129), channel_id=1, source_target_pairs={{0,1},{1,2},{2,3},{3,4},{4,5},{5,6},{6,7},{7,8},{8,9},{9,10},{10,1... | collective-permute-start | bytes 165896 | tf_op jit(solution)/shard_map/ppermute | solution.py:18
  82.0 88.3 %copy-start.3 = (f32[384,384]{1,0:T(8,128)S(1)}, f32[384,384]{1,0:T(8,128)}, u32[]{:S(2)}) copy-start(f32[384,384]{1,0:T(8,128)} %copy-done.2) | copy-start | bytes 1769476
  82.0 88.3 %copy-start.16 = (f32[384]{0:T(512)S(1)}, f32[384]{0:T(512)}, u32[]{:S(2)}) copy-start(f32[384]{0:T(512)} %copy-done.15) | copy-start | bytes 4612
  82.0 88.3 %copy-start.18 = (f32[384]{0:T(512)S(1)}, f32[384]{0:T(512)}, u32[]{:S(2)}) copy-start(f32[384]{0:T(512)} %copy-done.17) | copy-start | bytes 4612
  82.0 88.3 %copy-start.20 = (f32[384]{0:T(512)S(1)}, f32[384]{0:T(512)}, u32[]{:S(2)}) copy-start(f32[384]{0:T(512)} %copy-done.19) | copy-start | bytes 4612
  82.0 88.3 %copy-start.22 = (f32[384]{0:T(512)S(1)}, f32[384]{0:T(512)}, u32[]{:S(2)}) copy-start(f32[384]{0:T(512)} %copy-done.21) | copy-start | bytes 4612
  82.0 88.3 %copy-start.24 = (f32[384]{0:T(512)S(1)}, f32[384]{0:T(512)}, u32[]{:S(2)}) copy-start(f32[384]{0:T(512)} %copy-done.23) | copy-start | bytes 4612
  82.1 88.3 %copy-start.26 = (f32[384]{0:T(512)S(1)}, f32[384]{0:T(512)}, u32[]{:S(2)}) copy-start(f32[384]{0:T(512)} %copy-done.25) | copy-start | bytes 4612
  82.1 88.3 %copy-start.28 = (f32[384]{0:T(512)S(1)}, f32[384]{0:T(512)}, u32[]{:S(2)}) copy-start(f32[384]{0:T(512)} %copy-done.27) | copy-start | bytes 4612
  82.1 88.3 %copy-start.30 = (f32[384]{0:T(512)S(1)}, f32[384]{0:T(512)}, u32[]{:S(2)}) copy-start(f32[384]{0:T(512)} %copy-done.29) | copy-start | bytes 4612
  82.1 88.3 %copy-start.32 = (f32[384]{0:T(512)S(1)}, f32[384]{0:T(512)}, u32[]{:S(2)}) copy-start(f32[384]{0:T(512)} %copy-done.31) | copy-start | bytes 4612
  82.1 88.3 %copy-start.34 = (f32[384]{0:T(512)S(1)}, f32[384]{0:T(512)}, u32[]{:S(2)}) copy-start(f32[384]{0:T(512)} %copy-done.33) | copy-start | bytes 4612
  82.1 88.3 %copy-start.36 = (f32[384]{0:T(512)S(1)}, f32[384]{0:T(512)}, u32[]{:S(2)}) copy-start(f32[384]{0:T(512)} %copy-done.35) | copy-start | bytes 4612
  82.1 88.3 %copy-start.38 = (f32[384]{0:T(512)S(1)}, f32[384]{0:T(512)}, u32[]{:S(2)}) copy-start(f32[384]{0:T(512)} %copy-done.37) | copy-start | bytes 4612
  82.1 88.3 %copy-start.40 = (f32[384]{0:T(512)S(1)}, f32[384]{0:T(512)}, u32[]{:S(2)}) copy-start(f32[384]{0:T(512)} %copy-done.39) | copy-start | bytes 4612
  82.1 88.3 %copy-start.42 = (f32[384]{0:T(512)S(1)}, f32[384]{0:T(512)}, u32[]{:S(2)}) copy-start(f32[384]{0:T(512)} %copy-done.41) | copy-start | bytes 4612
  82.1 88.3 %copy-start.44 = (f32[384]{0:T(512)S(1)}, f32[384]{0:T(512)}, u32[]{:S(2)}) copy-start(f32[384]{0:T(512)} %copy-done.43) | copy-start | bytes 4612
  82.2 88.3 %copy-start.46 = (f32[384]{0:T(512)S(1)}, f32[384]{0:T(512)}, u32[]{:S(2)}) copy-start(f32[384]{0:T(512)} %copy-done.45) | copy-start | bytes 4612
  82.2 88.3 %copy-start.48 = (f32[384]{0:T(512)S(1)}, f32[384]{0:T(512)}, u32[]{:S(2)}) copy-start(f32[384]{0:T(512)} %copy-done.47) | copy-start | bytes 4612
  82.2 88.3 %copy-start.49 = (f32[384]{0:T(512)S(1)}, f32[384]{0:T(512)}, u32[]{:S(2)}) copy-start(f32[384]{0:T(512)} %get-tuple-element.85) | copy-start | bytes 4612
  82.2 88.3 %copy-start.50 = (f32[384]{0:T(512)S(1)}, f32[384]{0:T(512)}, u32[]{:S(2)}) copy-start(f32[384]{0:T(512)} %get-tuple-element.86) | copy-start | bytes 4612
  82.2 88.3 %copy-start.51 = (f32[384]{0:T(512)S(1)}, f32[384]{0:T(512)}, u32[]{:S(2)}) copy-start(f32[384]{0:T(512)} %get-tuple-element.87) | copy-start | bytes 4612
  82.2 88.3 %copy-start.52 = (f32[384]{0:T(512)S(1)}, f32[384]{0:T(512)}, u32[]{:S(2)}) copy-start(f32[384]{0:T(512)} %get-tuple-element.88) | copy-start | bytes 4612
  82.2 88.3 %copy-start.53 = (f32[384]{0:T(512)S(1)}, f32[384]{0:T(512)}, u32[]{:S(2)}) copy-start(f32[384]{0:T(512)} %get-tuple-element.89) | copy-start | bytes 4612
  82.2 88.3 %copy-start.54 = (f32[384]{0:T(512)S(1)}, f32[384]{0:T(512)}, u32[]{:S(2)}) copy-start(f32[384]{0:T(512)} %get-tuple-element.90) | copy-start | bytes 4612
  82.2 88.3 %copy-start.55 = (f32[384]{0:T(512)S(1)}, f32[384]{0:T(512)}, u32[]{:S(2)}) copy-start(f32[384]{0:T(512)} %get-tuple-element.91) | copy-start | bytes 4612
  82.2 88.3 %copy-start.56 = (f32[384]{0:T(512)S(1)}, f32[384]{0:T(512)}, u32[]{:S(2)}) copy-start(f32[384]{0:T(512)} %get-tuple-element.92) | copy-start | bytes 4612
  82.3 88.3 %copy-start.57 = (f32[384]{0:T(512)S(1)}, f32[384]{0:T(512)}, u32[]{:S(2)}) copy-start(f32[384]{0:T(512)} %get-tuple-element.93) | copy-start | bytes 4612
  83.4 86.7 %collective-permute-start.3 = (bf16[2,12,3,384]{3,2,1,0:T(4,128)(2,1)S(1)}, bf16[2,12,3,384]{3,2,1,0:T(4,128)(2,1)S(1)}, u32[]{:S(2)}, u32[]{:S(2)}) collective-permute-start(bf16[2,12,3,384]{3,2,1,0:T(4,128)(2,1)S(1)} %get-tuple-element.128), channel_id=1, source_target_pairs={{1,0},{2,1},{3,2},{4,3},{5,4},{6,5},{7,6},{8,7},{9,8},{10,9},{11,1... | collective-permute-start | bytes 165896 | tf_op jit(solution)/shard_map/ppermute | solution.py:20
  89.7 80.4 %collective-permute-start.2 = (bf16[2,12,3,384]{3,2,1,0:T(4,128)(2,1)S(1)}, bf16[2,12,3,384]{3,2,1,0:T(4,128)(2,1)S(1)}, u32[]{:S(2)}, u32[]{:S(2)}) collective-permute-start(bf16[2,12,3,384]{3,2,1,0:T(4,128)(2,1)S(1)} %get-tuple-element.127), channel_id=1, source_target_pairs={{0,1},{1,2},{2,3},{3,4},{4,5},{5,6},{6,7},{7,8},{8,9},{9,10},{10,1... | collective-permute-start | bytes 165896 | tf_op jit(solution)/shard_map/ppermute | solution.py:18
  (65 other events, 1452.9 us)
Sparse Core Ops, SparseCore 0:
  82.8 268.2 all-reduce.5
where the time goes:
time: 367 us; the launch traced here: 365 us
  waiting for transfers between devices  175 us (48%)
  blocking collectives  89.5 us (24%)
  other arithmetic  31.2 us (9%)
  local copies, waits for them, and re-layouts  19.3 us (5%)
  starting transfers between devices  17.9 us (5%)
  between operations  16.5 us (4%)
  matrix products  15.7 us (4%)
    psum x1, waiting for transfers between devices, on_device(): lax.psum((g_expand, g_reduce, g_head, g_kernel, g_gain, ocean_total), ('e...  175 us
    psum x1, blocking collectives, on_device(): lax.psum((g_expand, g_reduce, g_head, g_kernel, g_gain, ocean_total), ('e...  79.2 us
    ppermute x2, starting transfers between devices, padded(): lax.ppermute(head, axis, [((i + 1) % count, i) for i in range(count)])  17.9 us
    all_gather x1, blocking collectives, score_gradient(): pooled_members = lax.all_gather(prediction, 'ens', axis=1, tiled=True)  10.2 us
  transfers between devices with their start and end apart: 5, of which 1 were waited for; matrix products, arithmetic and copies ran while one was open for 4% of the time, Pallas kernels for 0%

commit v1 on v0

v1 whole, which is shorter than its diff:
```python
import jax
import jax.numpy as jnp
from jax import lax
from jax.experimental import pallas as pl
from jax.experimental.pallas import tpu as pltpu
from jax.sharding import PartitionSpec as P

FAIR_WEIGHT = 0.95
SMOOTHING = 0.5
NORM_EPS = 1e-06
D = 384
FFN = 1536
LANES = 3
BLOCK = 512
BLOCKS = FFN // BLOCK
MEMBERS = 8
HALF = 2560
COUNT_BITS = 8
F32 = jnp.float32
BF16 = jnp.bfloat16


def grid_of(mesh):
    tiles = mesh.shape["tile"]
    side = 4 if tiles == 64 else 2
    return side, side, tiles // (side * side)


def dot(a, b, dims):
    return lax.dot_general(a, b, (dims, ((), ())), preferred_element_type=F32)


NN = ((1,), (0,))
NT = ((1,), (1,))
TN = ((0,), (0,))


class Place:
    def __init__(self, sizes):
        self.nx, self.ny, self.nzh = sizes
        self.nz = 2 * self.nzh
        self.tiles = self.nx * self.ny * self.nzh
        self.ens = lax.axis_index("ens")
        self.tile = lax.axis_index("tile")
        self.core = lax.rem(self.ens, 2)
        self.zl = lax.div(self.ens, 2)
        self.zh = lax.rem(self.tile, self.nzh)
        self.x = lax.rem(lax.div(self.tile, self.nzh), self.nx)
        self.y = lax.div(self.tile, self.nzh * self.nx)
        self.z = self.zh * 2 + self.zl

    def at(self, x, y, z, core):
        return (lax.rem(z, 2) * 2 + core, (y * self.nx + x) * self.nzh + lax.div(z, 2))

    def along_x(self, d):
        return self.at(lax.rem(self.x + d, self.nx), self.y, self.z, self.core)

    def along_y(self, d):
        return self.at(self.x, lax.rem(self.y + d, self.ny), self.z, self.core)

    def along_z(self, d):
        return self.at(self.x, self.y, lax.rem(self.z + d, self.nz), self.core)

    def other_core(self):
        return self.at(self.x, self.y, self.z, 1 - self.core)

    def along_tile(self, d):
        return (self.ens, lax.rem(self.tile + d + self.tiles, self.tiles))

    def along_ens(self, d):
        return (lax.rem(self.ens + d, 4), self.tile)

    def everyone(self):
        peers = [self.along_tile(1), self.along_tile(-1)]
        peers += [self.along_ens(d) for d in range(1, 4)]
        peers += [self.along_x(d) for d in range(1, self.nx)]
        peers += [self.along_y(d) for d in range(1, self.ny)]
        peers += [self.along_z(d) for d in range(1, self.nz)]
        return peers


def remote(src, dst, send, recv, to):
    return pltpu.make_async_remote_copy(
        src_ref=src,
        dst_ref=dst,
        send_sem=send,
        recv_sem=recv,
        device_id=to,
        device_id_type=pl.DeviceIdType.MESH,
    )


def chunks_of(rows, devices):
    tiles = rows // 16
    for each in range(1, tiles + 1):
        if tiles % each == 0 and tiles // each <= devices:
            return tiles // each, each * 16


class Reduce:
    def __init__(self, place, refs, out):
        self.p = place
        self.g, self.rc, self.s1, self.r1, self.s2, self.r2, self.sz, self.rz, self.oz, self.o, sems = refs
        self.out = out
        n = place.nx
        self.n, self.nz = n, place.nz
        self.c_rows = HALF // 2
        self.p_rows = self.c_rows // n
        self.q_rows = self.p_rows // n
        self.owners, self.z_rows = chunks_of(2 * self.q_rows, self.nz)
        self.send, self.recv = sems
        self.slots = 0
        self.pending = []

    def slot(self):
        self.slots += 1
        return self.slots - 1

    def copy(self, src, dst, to):
        s = self.slot()
        return remote(src, dst, self.send.at[s], self.recv.at[s], to)

    def first(self, h):
        return self.p.x if h == 0 else self.p.y

    def second(self, h):
        return self.p.y if h == 0 else self.p.x

    def to_first(self, h, d):
        return self.p.along_x(d) if h == 0 else self.p.along_y(d)

    def to_second(self, h, d):
        return self.p.along_y(d) if h == 0 else self.p.along_x(d)

    def rows(self, start, count):
        return pl.ds(pl.multiple_of(start, 16), count)

    def start_core(self):
        other = 1 - self.p.core
        self.core_copies = [
            self.copy(
                self.g.at[h, self.rows(other * self.c_rows, self.c_rows)], self.rc.at[h], self.p.other_core()
            )
            for h in range(2)
        ]
        for copy in self.core_copies:
            copy.start()

    def add(self, out, out_at, terms, count, step):
        def body(i, _):
            at = i * step
            total = None
            for ref, start in terms:
                part = ref[self.rows(start + at, step), :].astype(F32)
                total = part if total is None else total + part
            out[self.rows(out_at + at, step), :] = total.astype(BF16)
            return 0

        lax.fori_loop(0, count // step, body, 0)

    def core_to_first(self):
        mine = self.p.core * self.c_rows
        self.first_copies = []
        for h in range(2):
            self.core_copies[h].wait_recv()
            self.add(self.s1.at[h], 0, [(self.g.at[h], mine), (self.rc.at[h], 0)], self.c_rows, 160)
            for d in range(1, self.n):
                target = lax.rem(self.first(h) + d, self.n)
                copy = self.copy(
                    self.s1.at[h, self.rows(target * self.p_rows, self.p_rows)],
                    self.r1.at[h, d - 1],
                    self.to_first(h, d),
                )
                copy.start()
                self.first_copies.append(copy)

    def first_to_second(self):
        self.second_copies = []
        per = self.n - 1
        for h in range(2):
            for d in range(per):
                self.first_copies[h * per + d].wait_recv()
            terms = [(self.s1.at[h], self.first(h) * self.p_rows)]
            terms += [(self.r1.at[h, d], 0) for d in range(per)]
            self.add(self.s2.at[h], 0, terms, self.p_rows, 80)
            for d in range(1, self.n):
                target = lax.rem(self.second(h) + d, self.n)
                copy = self.copy(
                    self.s2.at[h, self.rows(target * self.q_rows, self.q_rows)],
                    self.r2.at[h, d - 1],
                    self.to_second(h, d),
                )
                copy.start()
                self.second_copies.append(copy)

    def second_to_z(self):
        per = self.n - 1
        for h in range(2):
            for d in range(per):
                self.second_copies[h * per + d].wait_recv()
            terms = [(self.s2.at[h], self.second(h) * self.q_rows)]
            terms += [(self.r2.at[h, d], 0) for d in range(per)]
            self.add(self.sz, h * self.q_rows, terms, self.q_rows, 80)
        self.z_copies = []
        for d in range(1, self.nz):
            target = lax.rem(self.p.z + d, self.nz)
            copy = self.copy(
                self.sz.at[self.rows(lax.rem(target, self.owners) * self.z_rows, self.z_rows)],
                self.rz.at[d - 1],
                self.p.along_z(d),
            )
            self.z_copies.append(copy)
            pl.when(target < self.owners)(copy.start)

    def z_to_gather(self):
        is_owner = self.p.z < self.owners
        at = lax.rem(self.p.z, self.owners) * self.z_rows
        base = self.slots
        self.slots += self.nz
        self.gather_copies = [
            remote(
                self.oz.at[self.rows(at, self.z_rows)],
                self.oz.at[self.rows(at, self.z_rows)],
                self.send.at[base + d],
                self.recv.at[base + self.p.z],
                self.p.along_z(d),
            )
            for d in range(1, self.nz)
        ]
        self.gather_waits = [
            remote(
                self.oz.at[pl.ds(k * self.z_rows, self.z_rows)],
                self.oz.at[pl.ds(k * self.z_rows, self.z_rows)],
                self.send.at[base],
                self.recv.at[base + k],
                self.p.along_z(1),
            )
            for k in range(self.owners)
        ]

        @pl.when(is_owner)
        def _():
            for copy in self.z_copies:
                copy.wait_recv()
            terms = [(self.sz, at)] + [(self.rz.at[d], 0) for d in range(self.nz - 1)]
            self.add(self.oz, at, terms, self.z_rows, self.z_rows)
            for copy in self.gather_copies:
                copy.start()

    def shard(self, h):
        return self.p.core * self.c_rows + self.first(h) * self.p_rows + self.second(h) * self.q_rows

    def gather_to_second(self):
        for k in range(self.owners):
            pl.when(self.p.z != k)(self.gather_waits[k].wait_recv)
        self.back_second = []
        for h in range(2):
            at = self.shard(h)
            for d in range(1, self.n):
                copy = self.copy(
                    self.oz.at[pl.ds(h * self.q_rows, self.q_rows)],
                    self.o.at[h, self.rows(at, self.q_rows)],
                    self.to_second(h, d),
                )
                copy.start()
                self.back_second.append(copy)
        for h in range(2):
            self.o[h, self.rows(self.shard(h), self.q_rows), :] = self.oz[
                h * self.q_rows : (h + 1) * self.q_rows, :
            ]

    def second_to_first(self):
        per = self.n - 1
        self.back_first = []
        for h in range(2):
            for d in range(per):
                self.back_second[h * per + d].wait_recv()
            at = self.p.core * self.c_rows + self.first(h) * self.p_rows
            for d in range(1, self.n):
                copy = self.copy(
                    self.o.at[h, self.rows(at, self.p_rows)],
                    self.o.at[h, self.rows(at, self.p_rows)],
                    self.to_first(h, d),
                )
                copy.start()
                self.back_first.append(copy)

    def first_to_core(self):
        per = self.n - 1
        self.back_core = []
        self.local = []
        for h in range(2):
            for d in range(per):
                self.back_first[h * per + d].wait_recv()
            at = self.rows(self.p.core * self.c_rows, self.c_rows)
            copy = self.copy(self.o.at[h, at], self.out.at[h, at], self.p.other_core())
            copy.start()
            self.back_core.append(copy)
            keep = pltpu.make_async_copy(self.o.at[h, at], self.out.at[h, at], self.send.at[self.slot()])
            keep.start()
            self.local.append(keep)

    def finish(self):
        for copy in self.back_core:
            copy.wait_recv()
        for copy in self.local:
            copy.wait()
        for copy in self.core_copies + self.first_copies + self.second_copies:
            copy.wait_send()
        for d in range(1, self.nz):
            target = lax.rem(self.p.z + d, self.nz)
            pl.when(target < self.owners)(self.z_copies[d - 1].wait_send)

        @pl.when(self.p.z < self.owners)
        def _():
            for copy in self.gather_copies:
                copy.wait_send()

        for copy in self.back_second + self.back_first + self.back_core:
            copy.wait_send()


def reduce_scratch(sizes):
    n, _, nzh = sizes
    nz = 2 * nzh
    c_rows = HALF // 2
    p_rows = c_rows // n
    q_rows = p_rows // n
    _, z_rows = chunks_of(2 * q_rows, nz)
    slots = 2 + 4 * (n - 1) + nz - 1 + nz + 4 * (n - 1) + 4
    return [
        pltpu.VMEM((2, HALF, 128), BF16),
        pltpu.VMEM((2, c_rows, 128), BF16),
        pltpu.VMEM((2, c_rows, 128), BF16),
        pltpu.VMEM((2, n - 1, p_rows, 128), BF16),
        pltpu.VMEM((2, p_rows, 128), BF16),
        pltpu.VMEM((2, n - 1, q_rows, 128), BF16),
        pltpu.VMEM((2 * q_rows, 128), BF16),
        pltpu.VMEM((nz - 1, z_rows, 128), BF16),
        pltpu.VMEM((2 * q_rows, 128), BF16),
        pltpu.VMEM((2, HALF, 128), BF16),
        (pltpu.SemaphoreType.DMA((slots,)), pltpu.SemaphoreType.DMA((slots,))),
    ]


def slope_of(offset):
    return offset * lax.rsqrt(offset * offset + SMOOTHING * SMOOTHING)


def put_main(batch, flat, value):
    count = value.shape[0]
    if flat < HALF:
        take = min(count, HALF - flat)
        batch[0, flat : flat + take, :] = value[:take].astype(BF16)
        if take < count:
            put_main(batch, HALF, value[take:])
        return
    for at in range(0, count, 64):
        shard = (flat - HALF + at) // 64
        batch[1, shard * 80 : shard * 80 + 64, :] = value[at : at + 64].astype(BF16)


def put_small(batch, index, value):
    batch[1, index * 80 + 64 : index * 80 + 80, :] = value.astype(BF16)


def work(sizes, *refs):
    (
        x_hbm, target_hbm, sea_hbm, kernel_hbm, gain_hbm, expand_hbm, reduce_hbm, head_hbm,
        out1, out2, direct_out,
        xb, tg, sea, taps, gain, we, wr, head,
        ext, dext, hs, hr, hs2, hr2, mixed, standard, recip, normed, before, slope, hidden, hidden_t, normed_t,
        block, head_t, fall, d_block, d_block_b, d_before, d_norm, gk,
        in_sems, halo_send, halo_recv, ens_send, ens_recv,
        *reduce_refs,
    ) = refs
    place = Place(sizes)
    pieces = len(reduce_refs) // 2
    first_refs = reduce_refs[: pieces - 2] + [tuple(reduce_refs[pieces - 2 : pieces])]
    second_refs = reduce_refs[pieces : 2 * pieces - 2] + [tuple(reduce_refs[2 * pieces - 2 :])]
    batch1 = Reduce(place, first_refs, out1)
    batch2 = Reduce(place, second_refs, out2)

    loads = [
        pltpu.make_async_copy(x_hbm.at[0, 0:8], xb.at[0:8], in_sems.at[0]),
        pltpu.make_async_copy(x_hbm.at[1, 0:8], xb.at[8:16], in_sems.at[1]),
        pltpu.make_async_copy(x_hbm.at[0, 8:12], xb.at[16:20], in_sems.at[2]),
        pltpu.make_async_copy(x_hbm.at[1, 8:12], xb.at[20:24], in_sems.at[3]),
    ]
    tap_loads = [
        pltpu.make_async_copy(kernel_hbm.at[:, :, l * 128 : (l + 1) * 128], taps.at[l], in_sems.at[4 + l])
        for l in range(LANES)
    ]
    later = [
        pltpu.make_async_copy(gain_hbm, gain, in_sems.at[7]),
        pltpu.make_async_copy(head_hbm, head, in_sems.at[8]),
        pltpu.make_async_copy(expand_hbm, we, in_sems.at[9]),
        pltpu.make_async_copy(reduce_hbm, wr, in_sems.at[10]),
        pltpu.make_async_copy(target_hbm, tg, in_sems.at[11]),
        pltpu.make_async_copy(sea_hbm, sea, in_sems.at[12]),
    ]
    for copy in loads + tap_loads + later:
        copy.start()

    barrier = pltpu.get_barrier_semaphore()
    peers = place.everyone()
    for peer in peers:
        pl.semaphore_signal(barrier, inc=1, device_id=peer, device_id_type=pl.DeviceIdType.MESH)

    def clear(i, _):
        l, m = lax.div(i, 2), lax.rem(i, 2)
        for ref in (ext, dext):
            ref[l, m, 0:3] = jnp.zeros((3, 32, 128), F32)
            ref[l, m, 15:18] = jnp.zeros((3, 32, 128), F32)
        return 0

    lax.fori_loop(0, 2 * LANES, clear, 0)
    gk[...] = jnp.zeros_like(gk)
    for copy in loads:
        copy.wait()
    for l in range(LANES):
        lanes = slice(l * 128, (l + 1) * 128)
        for m in range(2):
            ext[l, m, 3:11, 8:24, :] = xb[m * 8 : m * 8 + 8, :, lanes].astype(F32)
            ext[l, m, 11:15, 8:24, :] = xb[16 + m * 4 : 20 + m * 4, :, lanes].astype(F32)

    def pack(field, out):
        for side, col in ((0, 8), (1, 21)):
            for m in range(2):
                for j in range(3):
                    for l in range(LANES):
                        out[side, m * 3 + j, :, l * 128 : (l + 1) * 128] = field[l, m, 2:18, col + j, :].astype(BF16)

    def unpack(field, got):
        for side, col in ((0, 5), (1, 24)):
            for m in range(2):
                for j in range(3):
                    for l in range(LANES):
                        field[l, m, 2:18, col + j, :] = got[side, m * 3 + j, :, l * 128 : (l + 1) * 128].astype(F32)

    def halo(out, got, at):
        copies = [
            remote(out.at[0], got.at[1], halo_send.at[at], halo_recv.at[at], place.along_tile(-1)),
            remote(out.at[1], got.at[0], halo_send.at[at + 1], halo_recv.at[at + 1], place.along_tile(1)),
        ]
        for copy in copies:
            copy.start()
        return copies

    pack(ext, hs)
    pl.semaphore_wait(barrier, len(peers))
    halo1 = halo(hs, hr, 0)

    for copy in tap_loads + later:
        copy.wait()
    head_f = head[...].astype(F32).T
    head_t[...] = jnp.concatenate([head_f, jnp.zeros((80 - head_f.shape[0], D), F32)], axis=0).astype(BF16)
    for copy in halo1:
        copy.wait_recv()
    unpack(ext, hr)

    def correlate(field, l, m, flip):
        total = jnp.zeros((12, 16, 128), F32)
        for j in range(7):
            shifted = field[l, m, :, 5 + j : 21 + j, :]
            for i in range(7):
                tap = taps[l, 6 - i, 6 - j : 7 - j, :] if flip else taps[l, i, j : j + 1, :]
                total = total + shifted[i : i + 12] * tap
        return total

    def mix(i, _):
        l, m = lax.div(i, 2), lax.rem(i, 2)
        total = correlate(ext, l, m, False)
        mixed[l, pl.ds(m * 8, 8)] = total[:8]
        mixed[l, pl.ds(16 + m * 4, 4)] = total[8:]
        return 0

    lax.fori_loop(0, 2 * LANES, mix, 0)

    def norm(i, _):
        rows = pl.ds(pl.multiple_of(i * 64, 64), 64)
        parts = [mixed[l, pl.ds(i * 4, 4)].reshape(64, 128) for l in range(LANES)]
        mean = jnp.sum(parts[0] + parts[1] + parts[2], axis=-1, keepdims=True) / D
        centre = [part - mean for part in parts]
        square = centre[0] * centre[0] + centre[1] * centre[1] + centre[2] * centre[2]
        scale = lax.rsqrt(jnp.sum(square, axis=-1, keepdims=True) / D + NORM_EPS)
        recip[rows, :] = jnp.broadcast_to(scale, (64, 128))
        for l in range(LANES):
            lanes = slice(l * 128, (l + 1) * 128)
            value = centre[l] * scale
            standard[rows, lanes] = value
            normed[rows, lanes] = (value * gain[:, lanes]).astype(BF16)
        return 0

    lax.fori_loop(0, 6, norm, 0)

    total = xb[...].reshape(D, D).astype(F32)
    for b in range(BLOCKS):
        columns = slice(b * BLOCK, (b + 1) * BLOCK)
        before[...] = dot(normed[...], we[:, columns], NN)

        def gelu(i, _):
            rows = pl.ds(pl.multiple_of(i * 32, 32), 32)
            v = before[rows, :]
            square = v * v
            scale = 0.7978845608028654
            t = jnp.tanh(v * (scale + (scale * 0.044715) * square))
            half = 0.5 + 0.5 * t
            hidden[rows, columns] = (v * half).astype(BF16)
            slope[rows, columns] = half + (0.5 * v) * (1.0 - t * t) * (scale + (scale * 3 * 0.044715) * square)
            return 0

        lax.fori_loop(0, 12, gelu, 0)
        total = total + dot(hidden[:, columns], wr[columns, :], NN)
    block[...] = total.astype(BF16)

    own = dot(head_t[...], block[...], NT)
    fall[place.ens] = own
    ens_copies = [
        remote(fall.at[place.ens], fall.at[place.ens], ens_send.at[d], ens_recv.at[place.ens], place.along_ens(d))
        for d in range(1, 4)
    ]
    ens_waits = [
        remote(
            fall.at[lax.rem(place.ens + d, 4)],
            fall.at[lax.rem(place.ens + d, 4)],
            ens_send.at[0],
            ens_recv.at[lax.rem(place.ens + d, 4)],
            place.along_ens(d),
        )
        for d in range(1, 4)
    ]
    for copy in ens_copies:
        copy.start()
    normed_t[...] = normed[...].T
    for b in range(BLOCKS):
        hidden_t[b * BLOCK : (b + 1) * BLOCK, :] = hidden[:, b * BLOCK : (b + 1) * BLOCK].T
    for copy in ens_waits:
        copy.wait_recv()

    spread = jnp.zeros((80, D), F32)
    for s in range(4):
        theirs = fall[s]
        swapped = jnp.concatenate(
            [theirs[:, 128:256], theirs[:, 0:128], pltpu.roll(theirs[:, 256:384], 64, 1)], axis=1
        )
        spread = spread + slope_of(own - theirs) + slope_of(own - swapped)
    observed = jnp.concatenate([tg[:, 0:128], tg[:, 0:128], tg[:, 128:256]], axis=1)
    ocean = jnp.concatenate([sea[:, 0:128], sea[:, 0:128], sea[:, 128:256]], axis=1)[0:1]
    slopes = slope_of(own - observed) / MEMBERS - FAIR_WEIGHT / (MEMBERS * (MEMBERS - 1)) * spread
    slopes_b = (slopes * ocean).astype(BF16)

    grad_head = dot(slopes_b, block[...], NN)
    for r in range(5):
        for l in range(LANES):
            put_small(batch1.g, r * 3 + l, grad_head[r * 16 : r * 16 + 16, l * 128 : (l + 1) * 128])
    for index in range(15, 32):
        put_small(batch1.g, index, jnp.zeros((16, 128), F32))
    back = dot(slopes_b, head_t[...], TN)
    d_block[...] = back
    d_block_b[...] = back.astype(BF16)
    grad_reduce = dot(hidden_t[...], d_block_b[...], NN)
    for l in range(LANES):
        put_main(batch1.g, l * FFN, grad_reduce[:, l * 128 : (l + 1) * 128])
    batch1.start_core()

    d_normed = jnp.zeros((D, D), F32)
    for b in range(BLOCKS):
        columns = slice(b * BLOCK, (b + 1) * BLOCK)
        before[...] = dot(d_block_b[...], wr[columns, :], NT)

        def gate(i, _):
            rows = pl.ds(pl.multiple_of(i * 32, 32), 32)
            d_before[rows, :] = (before[rows, :] * slope[rows, columns]).astype(BF16)
            return 0

        lax.fori_loop(0, 12, gate, 0)
        grad_expand = dot(normed_t[...], d_before[...], NN)
        for l in range(BLOCK // 128):
            put_main(batch2.g, (b * (BLOCK // 128) + l) * D, grad_expand[:, l * 128 : (l + 1) * 128])
        d_normed = d_normed + dot(d_before[...], we[:, columns], NT)
        if b == 1:
            batch1.core_to_first()
    d_norm[...] = d_normed

    gk[0, 7:8, :] = jnp.zeros((1, 128), F32)

    def unnorm(i, _):
        rows = pl.ds(pl.multiple_of(i * 64, 64), 64)
        value = [d_norm[rows, l * 128 : (l + 1) * 128] for l in range(LANES)]
        std = [standard[rows, l * 128 : (l + 1) * 128] for l in range(LANES)]
        for l in range(LANES):
            gk[l, 7:8, :] += jnp.sum(value[l] * std[l], axis=0, keepdims=True)
        scaled = [value[l] * gain[:, l * 128 : (l + 1) * 128] for l in range(LANES)]
        mean = jnp.sum(scaled[0] + scaled[1] + scaled[2], axis=-1, keepdims=True) / D
        along = jnp.sum(scaled[0] * std[0] + scaled[1] * std[1] + scaled[2] * std[2], axis=-1, keepdims=True) / D
        for l in range(LANES):
            mixed[l, pl.ds(i * 4, 4)] = (recip[rows, :] * (scaled[l] - mean - std[l] * along)).reshape(4, 16, 128)
        return 0

    lax.fori_loop(0, 6, unnorm, 0)
    for l in range(LANES):
        for m in range(2):
            dext[l, m, 3:11, 8:24, :] = mixed[l, m * 8 : m * 8 + 8]
            dext[l, m, 11:15, 8:24, :] = mixed[l, 16 + m * 4 : 20 + m * 4]
    pack(dext, hs2)
    halo2 = halo(hs2, hr2, 2)
    batch1.first_to_second()

    def kernel_grad(l, _):
        for j in range(7):
            near = [ext[l, m, :, 5 + j : 21 + j, :] for m in range(2)]
            for i in range(7):
                part = jnp.zeros((16, 128), F32)
                for m in range(2):
                    part = part + jnp.sum(dext[l, m, 3:15, 8:24, :] * near[m][i : i + 12], axis=0)
                gk[l, i * 8 + j : i * 8 + j + 1, :] = jnp.sum(part, axis=0, keepdims=True)
        return 0

    lax.fori_loop(0, LANES, kernel_grad, 0)
    count = jnp.sum(sea[0:1, 0:192]).astype(jnp.int32)
    lane = lax.broadcasted_iota(jnp.int32, (1, 128), 1)
    bits = lax.bitwise_and(lax.shift_right_logical(jnp.broadcast_to(count, (1, 128)), jnp.minimum(lane, 31)), 1)
    gk[0, 15:16, :] = jnp.where(lane < COUNT_BITS, bits, 0).astype(F32)
    for r in range(4):
        for l in range(LANES):
            put_small(batch2.g, r * 3 + l, gk[l, r * 16 : r * 16 + 16, :])
    for index in range(12, 32):
        put_small(batch2.g, index, jnp.zeros((16, 128), F32))
    batch2.start_core()
    batch1.second_to_z()

    for copy in halo2:
        copy.wait_recv()
    unpack(dext, hr2)

    def mix_back(i, _):
        l, m = lax.div(i, 2), lax.rem(i, 2)
        mixed_back = correlate(dext, l, m, True)
        mixed[l, pl.ds(m * 8, 8)] = mixed_back[:8]
        mixed[l, pl.ds(16 + m * 4, 4)] = mixed_back[8:]
        return 0

    lax.fori_loop(0, 2, mix_back, 0)
    batch2.core_to_first()
    batch1.z_to_gather()
    lax.fori_loop(2, 4, mix_back, 0)
    batch1.gather_to_second()
    lax.fori_loop(4, 6, mix_back, 0)
    batch2.first_to_second()
    batch1.second_to_first()
    for l in range(LANES):
        lanes = slice(l * 128, (l + 1) * 128)
        mixed[l] = mixed[l] + d_block[:, lanes].reshape(24, 16, 128)
    direct = []
    for l in range(LANES):
        for m in range(2):
            lanes = slice(l * 128, (l + 1) * 128)
            at = (l * 2 + m) * 2
            direct.append(
                pltpu.make_async_copy(
                    mixed.at[l, m * 8 : m * 8 + 8], direct_out.at[m, 0:8, :, lanes], in_sems.at[at]
                )
            )
            direct.append(
                pltpu.make_async_copy(
                    mixed.at[l, 16 + m * 4 : 20 + m * 4], direct_out.at[m, 8:12, :, lanes], in_sems.at[at + 1]
                )
            )
    for copy in direct:
        copy.start()
    batch2.second_to_z()
    batch1.first_to_core()
    batch2.z_to_gather()
    batch2.gather_to_second()
    batch2.second_to_first()
    batch2.first_to_core()
    for copy in halo1 + halo2 + ens_copies:
        copy.wait_send()
    for copy in direct:
        copy.wait()
    batch1.finish()
    batch2.finish()


def finish(o1, o2, direct, g_inputs, g_kernel, g_gain, g_expand, g_reduce, g_head):
    def small(o, index):
        return o[1, index * 80 + 64 : index * 80 + 80, :].astype(F32)

    g_inputs[...] = direct[...]
    rows = [[small(o2, r * 3 + l) for l in range(LANES)] for r in range(4)]
    weight = lax.broadcasted_iota(jnp.int32, (1, 128), 1)
    weight = jnp.where(weight < COUNT_BITS, lax.shift_left(1, jnp.minimum(weight, 15)), 0).astype(F32)
    total = jnp.sum(rows[0][0][15:16] * weight, axis=-1, keepdims=True) / 4
    scale = 1.0 / total
    for l in range(LANES):
        lanes = slice(l * 128, (l + 1) * 128)
        for i in range(7):
            at = (i % 2) * 8
            g_kernel[i, :, lanes] = rows[i // 2][l][at : at + 7] * scale
        g_gain[:, lanes] = rows[0][l][7:8] * scale
    head = jnp.concatenate(
        [jnp.concatenate([small(o1, r * 3 + l) for l in range(LANES)], axis=1) for r in range(5)], axis=0
    )
    g_head[...] = (head * scale).T[:, : g_head.shape[1]]

    def main(o, flat, count):
        if flat < HALF:
            take = min(count, HALF - flat)
            yield 0, o[0, flat : flat + take, :]
            for at, rows in main(o, HALF, count - take) if take < count else ():
                yield take + at, rows
            return
        for at in range(0, count, 64):
            shard = (flat - HALF + at) // 64
            yield at, o[1, shard * 80 : shard * 80 + 64, :]

    for l in range(LANES):
        for at, rows in main(o1, l * FFN, FFN):
            g_reduce[at : at + rows.shape[0], l * 128 : (l + 1) * 128] = rows.astype(F32) * scale
    for l in range(FFN // 128):
        for at, rows in main(o2, l * D, D):
            g_expand[at : at + rows.shape[0], l * 128 : (l + 1) * 128] = rows.astype(F32) * scale


def on_device(sizes, inputs, target, land_sea, kernel, norm_gain, w_expand, w_reduce, head_weight):
    outputs = target.shape[0]
    observed = target.reshape(outputs, 192)
    observed = jnp.concatenate([observed, observed[:, 128:192]], axis=1)
    observed = jnp.pad(observed, ((0, 80 - outputs), (0, 0)))
    ocean = land_sea.reshape(1, 192).astype(F32)
    ocean = jnp.concatenate([ocean, ocean[:, 128:192]], axis=1)
    ocean = jnp.broadcast_to(ocean, (8, 256))
    anywhere = pl.BlockSpec(memory_space=pl.ANY)
    vmem = pltpu.VMEM
    scratch = [
        vmem((24, 16, D), BF16),
        vmem((80, 256), F32),
        vmem((8, 256), F32),
        vmem((LANES, 7, 7, 128), F32),
        vmem((1, D), F32),
        vmem((D, FFN), BF16),
        vmem((FFN, D), BF16),
        vmem((D, outputs), BF16),
        vmem((LANES, 2, 18, 32, 128), F32),
        vmem((LANES, 2, 18, 32, 128), F32),
        vmem((2, 6, 16, D), BF16),
        vmem((2, 6, 16, D), BF16),
        vmem((2, 6, 16, D), BF16),
        vmem((2, 6, 16, D), BF16),
        vmem((LANES, 24, 16, 128), F32),
        vmem((D, D), F32),
        vmem((D, 128), F32),
        vmem((D, D), BF16),
        vmem((D, BLOCK), F32),
        vmem((D, FFN), F32),
        vmem((D, FFN), BF16),
        vmem((FFN, D), BF16),
        vmem((D, D), BF16),
        vmem((D, D), BF16),
        vmem((80, D), BF16),
        vmem((4, 80, D), F32),
        vmem((D, D), F32),
        vmem((D, D), BF16),
        vmem((D, BLOCK), BF16),
        vmem((D, D), F32),
        vmem((LANES, 64, 128), F32),
        pltpu.SemaphoreType.DMA((13,)),
        pltpu.SemaphoreType.DMA((4,)),
        pltpu.SemaphoreType.DMA((4,)),
        pltpu.SemaphoreType.DMA((4,)),
        pltpu.SemaphoreType.DMA((4,)),
    ]
    batch = reduce_scratch(sizes)
    batch = batch[:-1] + list(batch[-1])
    scratch += batch + batch
    o1, o2, direct = pl.pallas_call(
        lambda *refs: work(sizes, *refs),
        out_shape=(
            jax.ShapeDtypeStruct((2, HALF, 128), BF16),
            jax.ShapeDtypeStruct((2, HALF, 128), BF16),
            jax.ShapeDtypeStruct(inputs.shape, F32),
        ),
        in_specs=[anywhere] * 8,
        out_specs=(anywhere,) * 3,
        scratch_shapes=scratch,
        compiler_params=pltpu.CompilerParams(
            collective_id=0, has_side_effects=True, vmem_limit_bytes=48 * 1024 * 1024
        ),
        name="block_pass",
    )(inputs, observed, ocean, kernel, norm_gain.reshape(1, D), w_expand, w_reduce, head_weight)
    g_inputs, g_kernel, g_gain, g_expand, g_reduce, g_head = pl.pallas_call(
        finish,
        out_shape=(
            jax.ShapeDtypeStruct(inputs.shape, F32),
            jax.ShapeDtypeStruct(kernel.shape, F32),
            jax.ShapeDtypeStruct((1, D), F32),
            jax.ShapeDtypeStruct(w_expand.shape, F32),
            jax.ShapeDtypeStruct(w_reduce.shape, F32),
            jax.ShapeDtypeStruct(head_weight.shape, F32),
        ),
        compiler_params=pltpu.CompilerParams(vmem_limit_bytes=32 * 1024 * 1024),
        name="finish",
    )(o1, o2, direct)
    return g_inputs, g_kernel, g_gain.reshape(D), g_expand, g_reduce, g_head


def solution(mesh):
    sizes = grid_of(mesh)
    return jax.shard_map(
        lambda *arrays: on_device(sizes, *arrays),
        mesh=mesh,
        in_specs=(
            P("ens", None, "tile", None),
            P(None, None, "tile"),
            P(None, "tile"),
            P(),
            P(),
            P(),
            P(),
            P(),
        ),
        out_specs=(P("ens", None, "tile", None), P(), P(), P(), P(), P()),
        check_vma=False,
    )
```

time: 367 us -> 99.5 us (0.27)
  waiting for transfers between devices: 175 us -> 0 us
  blocking collectives: 89.5 us -> 0 us
  Pallas kernels: 0 us -> 89.1 us
  other arithmetic: 31.2 us -> 1.45 us
  starting transfers between devices: 17.9 us -> 0 us
  between operations: 16.5 us -> 0.66 us
  matrix products: 15.7 us -> 0 us
  local copies, waits for them, and re-layouts: 19.3 us -> 7.9 us
    psum x1 -> x0, waiting for transfers between devices: 175 us -> none  [on_device(): lax.psum((g_expand, g_reduce, g_head, g_kernel, g_gain, ocean_total), ('e...]
    pallas_call x0 -> x2, Pallas kernels: none -> 89.1 us  [the longest x1 86.3 us: on_device(): pl.pallas_call(lambda *refs: work(sizes, *refs), out_shape=(jax.ShapeDtyp...]
    psum x1 -> x0, blocking collectives: 79.2 us -> none  [on_device(): lax.psum((g_expand, g_reduce, g_head, g_kernel, g_gain, ocean_total), ('e...]
    ppermute x4 -> x0, starting transfers between devices: 17.9 us -> none  [the longest x2 17.9 us: padded(): lax.ppermute(head, axis, [((i + 1) % count, i) for i in range(count)])]
    dot_general x9 -> x0, matrix products: 15.7 us -> none  [the longest x1 4.17 us: block_rows(): lax.dot_general(d_block_b, w_reduce, (((1,), (1,)), ((), ())), preferred_...]
    reduce_sum x7 -> x0, other arithmetic: 13.2 us -> none  [the longest x3 6.11 us: on_device(): jnp.sum(d_mixed * padded_field[:, lat_step:lat_step + height, lon_step:lo...]
    all_gather x1 -> x0, blocking collectives: 10.2 us -> none  [score_gradient(): pooled_members = lax.all_gather(prediction, 'ens', axis=1, tiled=True)]
    div x7 -> x0, other arithmetic: 7.76 us -> none  [the longest x1 3.4 us: on_device(): g_expand / ocean_total]
  transfers between devices with their start and end apart: 5 -> 0, of which waited for: 1 -> 0; matrix products, arithmetic and copies ran while one was open for 4% -> 0% of each run, Pallas kernels for 0% -> 0%
where the time goes in v1:
time: 99.5 us; the launch traced here: 99.1 us
  Pallas kernels  89.1 us (90%)
  local copies, waits for them, and re-layouts  7.9 us (8%)
  other arithmetic  1.45 us (1%)
    pallas_call x1, Pallas kernels, on_device(): pl.pallas_call(lambda *refs: work(sizes, *refs), out_shape=(jax.ShapeDtyp...  86.3 us
    unnamed x10, local copies, waits for them, and re-layouts  6.13 us
    pallas_call x1, Pallas kernels, on_device(): pl.pallas_call(finish, out_shape=(jax.ShapeDtypeStruct(inputs.shape, F32)...  2.8 us

profile of v1, /device:TPU:1, one launch (start us, length us, event | category | flops | bytes accessed | tf_op | source)
XLA Modules:
  0.0 99.1 jit_solution(1814654546650438949)
XLA Ops:
  0.6 0.7 reshape.36.refs_4_
  1.3 0.7 convert_element_type.16
  2.0 0.1 convert_element_type.17
  2.1 0.1 pad_maximum_fusion
  2.2 1.0 %copy.18 = f32[77,192]{1,0:T(8,128)S(1)} copy(f32[77,192]{0,1:T(8,128)} %bitcast.2) | data formatting | bytes 118272 | tf_op jit(solution)/shard_map/reshape | solution.py:728
  3.2 0.1 select_maximum_fusion.refs_1_
  3.3 1.0 copy.19.refs_7_
  4.2 0.0 copy-start
  4.2 1.3 %copy-done = bf16[384,1536]{1,0:T(8,128)(2,1)S(1)} copy-done((bf16[384,1536]{1,0:T(8,128)(2,1)S(1)}, bf16[384,1536]{1,0:T(8,128)(2,1)}, u32[]{:S(2)}) %copy-start) | copy-done | bytes 1179672
  5.5 0.0 copy-start.1
  5.5 1.3 %copy-done.1 = bf16[1536,384]{1,0:T(8,128)(2,1)S(1)} copy-done((bf16[1536,384]{1,0:T(8,128)(2,1)S(1)}, bf16[1536,384]{1,0:T(8,128)(2,1)}, u32[]{:S(2)}) %copy-start.1) | copy-done | bytes 1179672
  6.8 0.0 copy-start.2
  6.8 1.0 copy-done.2
  7.7 0.0 copy-start.3
  7.7 0.9 copy-done.3
  8.6 86.3 %block_pass.1 = (bf16[2,2560,128]{2,1,0:T(8,128)(2,1)S(1)}, bf16[2,2560,128]{2,1,0:T(8,128)(2,1)S(1)}, f32[2,12,16,384]{3,2,1,0:T(8,128)S(1)}) custom-call(bf16[2,12,16,384]{3,2,1,0:T(8,128)(2,1)S(1)} %copy-done.2, f32[80,256]{1,0:T(8,128)S(1)} %select_maximum_fusion.refs_1_, f32[8,256]{1,0:T(8,128)S(1)} %broadcast_in_dim.8.refs_2_, ...), custom_call_target="tpu_custom_call" | custom-call | tf_op jit(solution)/shard_map/block_pass/pallas_call | solution.py:777
  95.0 2.8 %finish.1 = (f32[2,12,16,384]{3,2,1,0:T(8,128)}, f32[7,7,384]{2,1,0:T(8,128)}, f32[1,384]{1,0:T(1,128)S(1)}, f32[384,1536]{1,0:T(8,128)}, f32[1536,384]{1,0:T(8,128)}, /*index=5*/f32[384,77]{1,0:T(8,128)S(1)}) custom-call(bf16[2,2560,128]{2,1,0:T(8,128)(2,1)S(1)} %get-tuple-element.15.o1, bf16[2,2560,128]{2,1,0:T(8,128)(2,1)S(1)} %get-tuple-element.16.o2, ...), custom_call_target="tpu_custom_call" | custom-call | tf_op jit(solution)/shard_map/finish/pallas_call | solution.py:792
  97.7 0.6 reduce
  98.3 0.8 copy.20
  (3 shorter events, 0.0 us)
Async XLA Ops:
  4.2 1.3 %copy-start = (bf16[384,1536]{1,0:T(8,128)(2,1)S(1)}, bf16[384,1536]{1,0:T(8,128)(2,1)}, u32[]{:S(2)}) copy-start(bf16[384,1536]{1,0:T(8,128)(2,1)} %refs_5_.1) | copy-start | bytes 3538948
  5.5 1.3 %copy-start.1 = (bf16[1536,384]{1,0:T(8,128)(2,1)S(1)}, bf16[1536,384]{1,0:T(8,128)(2,1)}, u32[]{:S(2)}) copy-start(bf16[1536,384]{1,0:T(8,128)(2,1)} %refs_6_.1) | copy-start | bytes 3538948
  6.8 1.0 copy-start.2
  7.7 0.9 copy-start.3

commit v2 on v1

--- a/solution.py
+++ b/solution.py
@@ -16,6 +16,7 @@
 MEMBERS = 8
 HALF = 2560
 COUNT_BITS = 8
+FEW = 96
 F32 = jnp.float32
 BF16 = jnp.bfloat16
 
@@ -100,7 +101,7 @@
 class Reduce:
     def __init__(self, place, refs, out):
         self.p = place
-        self.g, self.rc, self.s1, self.r1, self.s2, self.r2, self.sz, self.rz, self.oz, self.o, sems = refs
+        self.g, self.rc, self.s1, self.r1, self.s2, self.r2, self.sz, self.rz, self.oz, sems = refs
         self.out = out
         n = place.nx
         self.n, self.nz = n, place.nz
@@ -135,16 +136,22 @@
     def rows(self, start, count):
         return pl.ds(pl.multiple_of(start, 16), count)
 
+    def pieces(self, h):
+        return [lax.rem(self.first(h) + d, self.n) * self.p_rows for d in (*range(1, self.n), 0)]
+
     def start_core(self):
         other = 1 - self.p.core
-        self.core_copies = [
-            self.copy(
-                self.g.at[h, self.rows(other * self.c_rows, self.c_rows)], self.rc.at[h], self.p.other_core()
-            )
-            for h in range(2)
-        ]
-        for copy in self.core_copies:
-            copy.start()
+        self.core_copies = [[], []]
+        for k in range(self.n):
+            for h in range(2):
+                at = self.pieces(h)[k]
+                copy = self.copy(
+                    self.g.at[h, self.rows(other * self.c_rows + at, self.p_rows)],
+                    self.rc.at[h, self.rows(at, self.p_rows)],
+                    self.p.other_core(),
+                )
+                copy.start()
+                self.core_copies[h].append(copy)
 
     def add(self, out, out_at, terms, count, step):
         def body(i, _):
@@ -160,26 +167,26 @@
 
     def core_to_first(self):
         mine = self.p.core * self.c_rows
-        self.first_copies = []
-        for h in range(2):
-            self.core_copies[h].wait_recv()
-            self.add(self.s1.at[h], 0, [(self.g.at[h], mine), (self.rc.at[h], 0)], self.c_rows, 160)
-            for d in range(1, self.n):
-                target = lax.rem(self.first(h) + d, self.n)
+        self.first_copies = [[], []]
+        for k in range(self.n):
+            for h in range(2):
+                at = self.pieces(h)[k]
+                self.core_copies[h][k].wait_recv()
+                self.add(self.s1.at[h], at, [(self.g.at[h], mine + at), (self.rc.at[h], at)], self.p_rows, 80)
+                if k == self.n - 1:
+                    continue
                 copy = self.copy(
-                    self.s1.at[h, self.rows(target * self.p_rows, self.p_rows)],
-                    self.r1.at[h, d - 1],
-                    self.to_first(h, d),
+                    self.s1.at[h, self.rows(at, self.p_rows)], self.r1.at[h, k], self.to_first(h, k + 1)
                 )
                 copy.start()
-                self.first_copies.append(copy)
+                self.first_copies[h].append(copy)
 
     def first_to_second(self):
         self.second_copies = []
         per = self.n - 1
         for h in range(2):
-            for d in range(per):
-                self.first_copies[h * per + d].wait_recv()
+            for copy in self.first_copies[h]:
+                copy.wait_recv()
             terms = [(self.s1.at[h], self.first(h) * self.p_rows)]
             terms += [(self.r1.at[h, d], 0) for d in range(per)]
             self.add(self.s2.at[h], 0, terms, self.p_rows, 80)
@@ -254,58 +261,52 @@
         for k in range(self.owners):
             pl.when(self.p.z != k)(self.gather_waits[k].wait_recv)
         self.back_second = []
+        self.kept = []
         for h in range(2):
-            at = self.shard(h)
+            at = self.rows(self.shard(h), self.q_rows)
+            mine = self.oz.at[pl.ds(h * self.q_rows, self.q_rows)]
             for d in range(1, self.n):
-                copy = self.copy(
-                    self.oz.at[pl.ds(h * self.q_rows, self.q_rows)],
-                    self.o.at[h, self.rows(at, self.q_rows)],
-                    self.to_second(h, d),
-                )
+                copy = self.copy(mine, self.out.at[h, at], self.to_second(h, d))
                 copy.start()
                 self.back_second.append(copy)
-        for h in range(2):
-            self.o[h, self.rows(self.shard(h), self.q_rows), :] = self.oz[
-                h * self.q_rows : (h + 1) * self.q_rows, :
-            ]
+            keep = pltpu.make_async_copy(mine, self.out.at[h, at], self.send.at[self.slot()])
+            keep.start()
+            self.kept.append(keep)
+
+    def piece(self, h, at):
+        return self.out.at[h, self.rows(self.p.core * self.c_rows + at, self.p_rows)]
 
     def second_to_first(self):
         per = self.n - 1
         self.back_first = []
+        self.back_core = []
         for h in range(2):
             for d in range(per):
                 self.back_second[h * per + d].wait_recv()
-            at = self.p.core * self.c_rows + self.first(h) * self.p_rows
+            self.kept[h].wait()
+            mine = self.piece(h, self.first(h) * self.p_rows)
             for d in range(1, self.n):
-                copy = self.copy(
-                    self.o.at[h, self.rows(at, self.p_rows)],
-                    self.o.at[h, self.rows(at, self.p_rows)],
-                    self.to_first(h, d),
-                )
+                copy = self.copy(mine, mine, self.to_first(h, d))
                 copy.start()
                 self.back_first.append(copy)
+            copy = self.copy(mine, mine, self.p.other_core())
+            copy.start()
+            self.back_core.append(copy)
 
     def first_to_core(self):
         per = self.n - 1
-        self.back_core = []
-        self.local = []
-        for h in range(2):
-            for d in range(per):
-                self.back_first[h * per + d].wait_recv()
-            at = self.rows(self.p.core * self.c_rows, self.c_rows)
-            copy = self.copy(self.o.at[h, at], self.out.at[h, at], self.p.other_core())
-            copy.start()
-            self.back_core.append(copy)
-            keep = pltpu.make_async_copy(self.o.at[h, at], self.out.at[h, at], self.send.at[self.slot()])
-            keep.start()
-            self.local.append(keep)
+        for d in sorted(range(1, self.n), key=lambda d: min(d, self.n - d)):
+            for h in range(2):
+                self.back_first[h * per + d - 1].wait_recv()
+                came = self.piece(h, lax.rem(self.first(h) + self.n - d, self.n) * self.p_rows)
+                copy = self.copy(came, came, self.p.other_core())
+                copy.start()
+                self.back_core.append(copy)
 
     def finish(self):
         for copy in self.back_core:
             copy.wait_recv()
-        for copy in self.local:
-            copy.wait()
-        for copy in self.core_copies + self.first_copies + self.second_copies:
+        for copy in sum(self.core_copies + self.first_copies, []) + self.second_copies:
             copy.wait_send()
         for d in range(1, self.nz):
             target = lax.rem(self.p.z + d, self.nz)
@@ -317,6 +318,65 @@
                 copy.wait_send()
 
         for copy in self.back_second + self.back_first + self.back_core:
+            copy.wait_send()
+
+
+class Few:
+    def __init__(self, place, refs, out):
+        self.p = place
+        self.g, self.rc, self.sx, self.sy, self.sz, self.o, self.send, self.recv = refs
+        self.out = out
+        self.slots = 0
+        self.copies = []
+
+    def copy(self, src, dst, to):
+        s = self.slots
+        self.slots += 1
+        copy = remote(src, dst, self.send.at[s], self.recv.at[s], to)
+        copy.start()
+        self.copies.append(copy)
+        return copy
+
+    def start(self):
+        self.got = [self.copy(self.g.at[1 - self.p.core], self.rc, self.p.other_core())]
+
+    def spread(self, value, slots, at, along, size):
+        for copy in self.got:
+            copy.wait_recv()
+        slots[at] = value().astype(BF16)
+        self.got = [self.copy(slots.at[at], slots.at[at], along(d)) for d in range(1, size)]
+
+    def total(self, slots, size):
+        value = slots[0].astype(F32)
+        for s in range(1, size):
+            value = value + slots[s].astype(F32)
+        return value
+
+    def to_x(self):
+        p = self.p
+        self.spread(lambda: self.g[p.core].astype(F32) + self.rc[...].astype(F32), self.sx, p.x, p.along_x, p.nx)
+
+    def to_y(self):
+        p = self.p
+        self.spread(lambda: self.total(self.sx, p.nx), self.sy, p.y, p.along_y, p.ny)
+
+    def to_z(self):
+        p = self.p
+        self.spread(lambda: self.total(self.sy, p.ny), self.sz, p.z, p.along_z, p.nz)
+
+    def to_core(self):
+        for copy in self.got:
+            copy.wait_recv()
+        self.o[...] = self.total(self.sz, self.p.nz).astype(BF16)
+        self.keep = pltpu.make_async_copy(self.o, self.out.at[self.p.core], self.send.at[self.slots])
+        self.slots += 1
+        self.keep.start()
+        self.got = [self.copy(self.o, self.out.at[self.p.core], self.p.other_core())]
+
+    def finish(self):
+        self.got[0].wait_recv()
+        self.keep.wait()
+        for copy in self.copies:
             copy.wait_send()
 
 
@@ -327,7 +387,7 @@
     p_rows = c_rows // n
     q_rows = p_rows // n
     _, z_rows = chunks_of(2 * q_rows, nz)
-    slots = 2 + 4 * (n - 1) + nz - 1 + nz + 4 * (n - 1) + 4
+    slots = 2 * n + 4 * (n - 1) + nz - 1 + nz + 2 * (n - 1) + 2 + 2 * (n - 1) + 2 * n
     return [
         pltpu.VMEM((2, HALF, 128), BF16),
         pltpu.VMEM((2, c_rows, 128), BF16),
@@ -338,7 +398,6 @@
         pltpu.VMEM((2 * q_rows, 128), BF16),
         pltpu.VMEM((nz - 1, z_rows, 128), BF16),
         pltpu.VMEM((2 * q_rows, 128), BF16),
-        pltpu.VMEM((2, HALF, 128), BF16),
         (pltpu.SemaphoreType.DMA((slots,)), pltpu.SemaphoreType.DMA((slots,))),
     ]
 
@@ -364,22 +423,27 @@
     batch[1, index * 80 + 64 : index * 80 + 80, :] = value.astype(BF16)
 
 
+def put_few(batch, index, value):
+    batch[index // 6, index % 6 * 16 : index % 6 * 16 + 16, :] = value.astype(BF16)
+
+
 def work(sizes, *refs):
     (
         x_hbm, target_hbm, sea_hbm, kernel_hbm, gain_hbm, expand_hbm, reduce_hbm, head_hbm,
-        out1, out2, direct_out,
-        xb, tg, sea, taps, gain, we, wr, head,
-        ext, dext, hs, hr, hs2, hr2, mixed, standard, recip, normed, before, slope, hidden, hidden_t, normed_t,
+        out1, out2, out3, direct_out,
+        xb, target, tall, tg, sea, taps, gain, we, wr, head,
+        ext, dext, rim, hs, hr, hs2, hr2, mixed, standard, recip, normed, before, slope, hidden, hidden_t, normed_t,
         block, head_t, fall, d_block, d_block_b, d_before, d_norm, gk,
         in_sems, halo_send, halo_recv, ens_send, ens_recv,
-        *reduce_refs,
+        *rest,
     ) = refs
     place = Place(sizes)
-    pieces = len(reduce_refs) // 2
-    first_refs = reduce_refs[: pieces - 2] + [tuple(reduce_refs[pieces - 2 : pieces])]
-    second_refs = reduce_refs[pieces : 2 * pieces - 2] + [tuple(reduce_refs[2 * pieces - 2 :])]
-    batch1 = Reduce(place, first_refs, out1)
-    batch2 = Reduce(place, second_refs, out2)
+    few = Few(place, rest[-8:], out3)
+    pieces = (len(rest) - 8) // 2
+    batch1, batch2 = (
+        Reduce(place, [*mine[:-2], mine[-2:]], out)
+        for mine, out in ((rest[:pieces], out1), (rest[pieces : 2 * pieces], out2))
+    )
 
     loads = [
         pltpu.make_async_copy(x_hbm.at[0, 0:8], xb.at[0:8], in_sems.at[0]),
@@ -396,7 +460,7 @@
         pltpu.make_async_copy(head_hbm, head, in_sems.at[8]),
         pltpu.make_async_copy(expand_hbm, we, in_sems.at[9]),
         pltpu.make_async_copy(reduce_hbm, wr, in_sems.at[10]),
-        pltpu.make_async_copy(target_hbm, tg, in_sems.at[11]),
+        pltpu.make_async_copy(target_hbm, target, in_sems.at[11]),
         pltpu.make_async_copy(sea_hbm, sea, in_sems.at[12]),
     ]
     for copy in loads + tap_loads + later:
@@ -416,6 +480,7 @@
 
     lax.fori_loop(0, 2 * LANES, clear, 0)
     gk[...] = jnp.zeros_like(gk)
+    rim[...] = jnp.zeros_like(rim)
     for copy in loads:
         copy.wait()
     for l in range(LANES):
@@ -429,14 +494,18 @@
             for m in range(2):
                 for j in range(3):
                     for l in range(LANES):
-                        out[side, m * 3 + j, :, l * 128 : (l + 1) * 128] = field[l, m, 2:18, col + j, :].astype(BF16)
+                        rows = slice((m * 3 + j) * 12, (m * 3 + j) * 12 + 12)
+                        rim[side, rows, l * 128 : (l + 1) * 128] = field[l, m, 3:15, col + j, :]
+        out[...] = rim[...].astype(BF16)
 
     def unpack(field, got):
+        rim[...] = got[...].astype(F32)
         for side, col in ((0, 5), (1, 24)):
             for m in range(2):
                 for j in range(3):
                     for l in range(LANES):
-                        field[l, m, 2:18, col + j, :] = got[side, m * 3 + j, :, l * 128 : (l + 1) * 128].astype(F32)
+                        rows = slice((m * 3 + j) * 12, (m * 3 + j) * 12 + 12)
+                        field[l, m, 3:15, col + j, :] = rim[side, rows, l * 128 : (l + 1) * 128]
 
     def halo(out, got, at):
         copies = [
@@ -453,8 +522,17 @@
 
     for copy in tap_loads + later:
         copy.wait()
-    head_f = head[...].astype(F32).T
-    head_t[...] = jnp.concatenate([head_f, jnp.zeros((80 - head_f.shape[0], D), F32)], axis=0).astype(BF16)
+    outputs = head.shape[0]
+    head_t[...] = jnp.concatenate([head[...].astype(F32), jnp.zeros((80 - outputs, D), F32)], axis=0).astype(BF16)
+    diagonal = lax.broadcasted_iota(jnp.int32, (16, 16), 0) == lax.broadcasted_iota(jnp.int32, (16, 16), 1)
+    tall[...] = jnp.zeros_like(tall)
+    for a in range(12):
+        water = jnp.broadcast_to(sea[a : a + 1, :].astype(F32), (16, 16))
+        water = jnp.sum(jnp.where(diagonal, water, 0.0), axis=1, keepdims=True)
+        for at in (a * 16,) if a < 8 else (a * 16, a * 16 + 64):
+            tall[at : at + 16, 0:outputs] = target[a]
+            tall[at : at + 16, outputs : outputs + 1] = water
+    tg[...] = tall[...].T[0:80]
     for copy in halo1:
         copy.wait_recv()
     unpack(ext, hr)
@@ -476,6 +554,8 @@
         return 0
 
     lax.fori_loop(0, 2 * LANES, mix, 0)
+
+    gain_row = gain[...].reshape(1, D)
 
     def norm(i, _):
         rows = pl.ds(pl.multiple_of(i * 64, 64), 64)
@@ -489,7 +569,7 @@
             lanes = slice(l * 128, (l + 1) * 128)
             value = centre[l] * scale
             standard[rows, lanes] = value
-            normed[rows, lanes] = (value * gain[:, lanes]).astype(BF16)
+            normed[rows, lanes] = (value * gain_row[:, lanes]).astype(BF16)
         return 0
 
     lax.fori_loop(0, 6, norm, 0)
@@ -515,38 +595,39 @@
     block[...] = total.astype(BF16)
 
     own = dot(head_t[...], block[...], NT)
-    fall[place.ens] = own
-    ens_copies = [
-        remote(fall.at[place.ens], fall.at[place.ens], ens_send.at[d], ens_recv.at[place.ens], place.along_ens(d))
-        for d in range(1, 4)
+    fall[0] = own
+    far = place.along_ens(2)
+    far_copies = [
+        remote(fall.at[0, pl.ds(r, 40)], fall.at[2, pl.ds(r, 40)], ens_send.at[k], ens_recv.at[k], far)
+        for k, r in enumerate((0, 40))
     ]
-    ens_waits = [
-        remote(
-            fall.at[lax.rem(place.ens + d, 4)],
-            fall.at[lax.rem(place.ens + d, 4)],
-            ens_send.at[0],
-            ens_recv.at[lax.rem(place.ens + d, 4)],
-            place.along_ens(d),
-        )
-        for d in range(1, 4)
+    near_copy = remote(fall.at[0], fall.at[1], ens_send.at[2], ens_recv.at[2], place.other_core())
+    relays = [
+        remote(fall.at[2, pl.ds(r, 40)], fall.at[3, pl.ds(r, 40)], ens_send.at[3 + k], ens_recv.at[3 + k], place.other_core())
+        for k, r in enumerate((0, 40))
     ]
-    for copy in ens_copies:
+    for copy in [*far_copies, near_copy]:
         copy.start()
     normed_t[...] = normed[...].T
     for b in range(BLOCKS):
         hidden_t[b * BLOCK : (b + 1) * BLOCK, :] = hidden[:, b * BLOCK : (b + 1) * BLOCK].T
-    for copy in ens_waits:
-        copy.wait_recv()
+    for came, relay in zip(far_copies, relays):
+        came.wait_recv()
+        relay.start()
+    near_copy.wait_recv()
 
     spread = jnp.zeros((80, D), F32)
     for s in range(4):
+        if s == 3:
+            for copy in relays:
+                copy.wait_recv()
         theirs = fall[s]
         swapped = jnp.concatenate(
             [theirs[:, 128:256], theirs[:, 0:128], pltpu.roll(theirs[:, 256:384], 64, 1)], axis=1
         )
         spread = spread + slope_of(own - theirs) + slope_of(own - swapped)
     observed = jnp.concatenate([tg[:, 0:128], tg[:, 0:128], tg[:, 128:256]], axis=1)
-    ocean = jnp.concatenate([sea[:, 0:128], sea[:, 0:128], sea[:, 128:256]], axis=1)[0:1]
+    ocean = observed[outputs : outputs + 1]
     slopes = slope_of(own - observed) / MEMBERS - FAIR_WEIGHT / (MEMBERS * (MEMBERS - 1)) * spread
     slopes_b = (slopes * ocean).astype(BF16)
 
@@ -554,8 +635,10 @@
     for r in range(5):
         for l in range(LANES):
             put_small(batch1.g, r * 3 + l, grad_head[r * 16 : r * 16 + 16, l * 128 : (l + 1) * 128])
-    for index in range(15, 32):
-        put_small(batch1.g, index, jnp.zeros((16, 128), F32))
+    for index in range(32):
+        if index >= 15:
+            put_small(batch1.g, index, jnp.zeros((16, 128), F32))
+        put_small(batch2.g, index, jnp.zeros((16, 128), F32))
     back = dot(slopes_b, head_t[...], TN)
     d_block[...] = back
     d_block_b[...] = back.astype(BF16)
@@ -581,6 +664,7 @@
         d_normed = d_normed + dot(d_before[...], we[:, columns], NT)
         if b == 1:
             batch1.core_to_first()
+    batch2.start_core()
     d_norm[...] = d_normed
 
     gk[0, 7:8, :] = jnp.zeros((1, 128), F32)
@@ -591,7 +675,7 @@
         std = [standard[rows, l * 128 : (l + 1) * 128] for l in range(LANES)]
         for l in range(LANES):
             gk[l, 7:8, :] += jnp.sum(value[l] * std[l], axis=0, keepdims=True)
-        scaled = [value[l] * gain[:, l * 128 : (l + 1) * 128] for l in range(LANES)]
+        scaled = [value[l] * gain_row[:, l * 128 : (l + 1) * 128] for l in range(LANES)]
         mean = jnp.sum(scaled[0] + scaled[1] + scaled[2], axis=-1, keepdims=True) / D
         along = jnp.sum(scaled[0] * std[0] + scaled[1] * std[1] + scaled[2] * std[2], axis=-1, keepdims=True) / D
         for l in range(LANES):
@@ -605,7 +689,6 @@
             dext[l, m, 11:15, 8:24, :] = mixed[l, 16 + m * 4 : 20 + m * 4]
     pack(dext, hs2)
     halo2 = halo(hs2, hr2, 2)
-    batch1.first_to_second()
 
     def kernel_grad(l, _):
         for j in range(7):
@@ -617,19 +700,19 @@
                 gk[l, i * 8 + j : i * 8 + j + 1, :] = jnp.sum(part, axis=0, keepdims=True)
         return 0
 
-    lax.fori_loop(0, LANES, kernel_grad, 0)
-    count = jnp.sum(sea[0:1, 0:192]).astype(jnp.int32)
+    lax.fori_loop(0, 2, kernel_grad, 0)
+    batch2.core_to_first()
+    lax.fori_loop(2, 3, kernel_grad, 0)
+    count = jnp.sum(sea[...].astype(F32)).astype(jnp.int32)
     lane = lax.broadcasted_iota(jnp.int32, (1, 128), 1)
     bits = lax.bitwise_and(lax.shift_right_logical(jnp.broadcast_to(count, (1, 128)), jnp.minimum(lane, 31)), 1)
     gk[0, 15:16, :] = jnp.where(lane < COUNT_BITS, bits, 0).astype(F32)
     for r in range(4):
         for l in range(LANES):
-            put_small(batch2.g, r * 3 + l, gk[l, r * 16 : r * 16 + 16, :])
-    for index in range(12, 32):
-        put_small(batch2.g, index, jnp.zeros((16, 128), F32))
-    batch2.start_core()
-    batch1.second_to_z()
-
+            put_few(few.g, r * 3 + l, gk[l, r * 16 : r * 16 + 16, :])
+    few.start()
+    batch1.first_to_second()
+    few.to_x()
     for copy in halo2:
         copy.wait_recv()
     unpack(dext, hr2)
@@ -641,14 +724,11 @@
         mixed[l, pl.ds(16 + m * 4, 4)] = mixed_back[8:]
         return 0
 
-    lax.fori_loop(0, 2, mix_back, 0)
-    batch2.core_to_first()
-    batch1.z_to_gather()
-    lax.fori_loop(2, 4, mix_back, 0)
-    batch1.gather_to_second()
+    lax.fori_loop(0, 4, mix_back, 0)
+    batch1.second_to_z()
+    few.to_y()
+    batch2.first_to_second()
     lax.fori_loop(4, 6, mix_back, 0)
-    batch2.first_to_second()
-    batch1.second_to_first()
     for l in range(LANES):
         lanes = slice(l * 128, (l + 1) * 128)
         mixed[l] = mixed[l] + d_block[:, lanes].reshape(24, 16, 128)
@@ -670,25 +750,34 @@
     for copy in direct:
         copy.start()
     batch2.second_to_z()
-    batch1.first_to_core()
+    batch1.z_to_gather()
+    few.to_z()
     batch2.z_to_gather()
+    batch1.gather_to_second()
+    few.to_core()
+    batch1.second_to_first()
     batch2.gather_to_second()
     batch2.second_to_first()
+    batch1.first_to_core()
     batch2.first_to_core()
-    for copy in halo1 + halo2 + ens_copies:
+    for copy in halo1 + halo2 + far_copies + [near_copy] + relays:
         copy.wait_send()
     for copy in direct:
         copy.wait()
+    few.finish()
     batch1.finish()
     batch2.finish()
 
 
-def finish(o1, o2, direct, g_inputs, g_kernel, g_gain, g_expand, g_reduce, g_head):
+def finish(o1, o2, o3, direct, g_inputs, g_kernel, g_gain, g_expand, g_reduce, g_head):
     def small(o, index):
         return o[1, index * 80 + 64 : index * 80 + 80, :].astype(F32)
 
     g_inputs[...] = direct[...]
-    rows = [[small(o2, r * 3 + l) for l in range(LANES)] for r in range(4)]
+    def few(index):
+        return o3[index // 6, index % 6 * 16 : index % 6 * 16 + 16, :].astype(F32)
+
+    rows = [[few(r * 3 + l) for l in range(LANES)] for r in range(4)]
     weight = lax.broadcasted_iota(jnp.int32, (1, 128), 1)
     weight = jnp.where(weight < COUNT_BITS, lax.shift_left(1, jnp.minimum(weight, 15)), 0).astype(F32)
     total = jnp.sum(rows[0][0][15:16] * weight, axis=-1, keepdims=True) / 4
@@ -698,11 +787,11 @@
         for i in range(7):
             at = (i % 2) * 8
             g_kernel[i, :, lanes] = rows[i // 2][l][at : at + 7] * scale
-        g_gain[:, lanes] = rows[0][l][7:8] * scale
+        g_gain[lanes] = (rows[0][l][7:8] * scale).reshape(128)
     head = jnp.concatenate(
         [jnp.concatenate([small(o1, r * 3 + l) for l in range(LANES)], axis=1) for r in range(5)], axis=0
     )
-    g_head[...] = (head * scale).T[:, : g_head.shape[1]]
+    g_head[...] = (head * scale)[: g_head.shape[0]]
 
     def main(o, flat, count):
         if flat < HALF:
@@ -725,29 +814,29 @@
 
 def on_device(sizes, inputs, target, land_sea, kernel, norm_gain, w_expand, w_reduce, head_weight):
     outputs = target.shape[0]
-    observed = target.reshape(outputs, 192)
-    observed = jnp.concatenate([observed, observed[:, 128:192]], axis=1)
-    observed = jnp.pad(observed, ((0, 80 - outputs), (0, 0)))
-    ocean = land_sea.reshape(1, 192).astype(F32)
-    ocean = jnp.concatenate([ocean, ocean[:, 128:192]], axis=1)
-    ocean = jnp.broadcast_to(ocean, (8, 256))
+    by_cell = jnp.transpose(target, (1, 2, 0))
+    head_rows = head_weight.T
     anywhere = pl.BlockSpec(memory_space=pl.ANY)
+    in_hbm = pl.BlockSpec(memory_space=pltpu.HBM)
     vmem = pltpu.VMEM
     scratch = [
         vmem((24, 16, D), BF16),
+        vmem((12, 16, outputs), F32),
+        vmem((256, 128), F32),
         vmem((80, 256), F32),
-        vmem((8, 256), F32),
+        vmem((12, 16), jnp.int32),
         vmem((LANES, 7, 7, 128), F32),
-        vmem((1, D), F32),
+        vmem((D,), F32),
         vmem((D, FFN), BF16),
         vmem((FFN, D), BF16),
-        vmem((D, outputs), BF16),
+        vmem((outputs, D), BF16),
         vmem((LANES, 2, 18, 32, 128), F32),
         vmem((LANES, 2, 18, 32, 128), F32),
-        vmem((2, 6, 16, D), BF16),
-        vmem((2, 6, 16, D), BF16),
-        vmem((2, 6, 16, D), BF16),
-        vmem((2, 6, 16, D), BF16),
+        vmem((2, 80, D), F32),
+        vmem((2, 80, D), BF16),
+        vmem((2, 80, D), BF16),
+        vmem((2, 80, D), BF16),
+        vmem((2, 80, D), BF16),
         vmem((LANES, 24, 16, 128), F32),
         vmem((D, D), F32),
         vmem((D, 128), F32),
@@ -768,41 +857,48 @@
         pltpu.SemaphoreType.DMA((13,)),
         pltpu.SemaphoreType.DMA((4,)),
         pltpu.SemaphoreType.DMA((4,)),
-        pltpu.SemaphoreType.DMA((4,)),
-        pltpu.SemaphoreType.DMA((4,)),
+        pltpu.SemaphoreType.DMA((5,)),
+        pltpu.SemaphoreType.DMA((5,)),
     ]
     batch = reduce_scratch(sizes)
     batch = batch[:-1] + list(batch[-1])
     scratch += batch + batch
-    o1, o2, direct = pl.pallas_call(
+    scratch += [vmem((2, FEW, 128), BF16), vmem((FEW, 128), BF16)]
+    scratch += [vmem((count, FEW, 128), BF16) for count in (sizes[0], sizes[1], 2 * sizes[2])]
+    few_slots = 2 + sizes[0] + sizes[1] + 2 * sizes[2]
+    scratch += [vmem((FEW, 128), BF16), pltpu.SemaphoreType.DMA((few_slots,)), pltpu.SemaphoreType.DMA((few_slots,))]
+    operands = [inputs, by_cell, land_sea, kernel, norm_gain, w_expand, w_reduce, head_rows]
+    operands = [pltpu.with_memory_space_constraint(operand, pltpu.HBM) for operand in operands]
+    o1, o2, o3, direct = pl.pallas_call(
         lambda *refs: work(sizes, *refs),
         out_shape=(
             jax.ShapeDtypeStruct((2, HALF, 128), BF16),
             jax.ShapeDtypeStruct((2, HALF, 128), BF16),
+            jax.ShapeDtypeStruct((2, FEW, 128), BF16),
             jax.ShapeDtypeStruct(inputs.shape, F32),
         ),
-        in_specs=[anywhere] * 8,
-        out_specs=(anywhere,) * 3,
+        in_specs=[in_hbm] * 8,
+        out_specs=(anywhere,) * 4,
         scratch_shapes=scratch,
         compiler_params=pltpu.CompilerParams(
             collective_id=0, has_side_effects=True, vmem_limit_bytes=48 * 1024 * 1024
         ),
         name="block_pass",
-    )(inputs, observed, ocean, kernel, norm_gain.reshape(1, D), w_expand, w_reduce, head_weight)
+    )(*operands)
     g_inputs, g_kernel, g_gain, g_expand, g_reduce, g_head = pl.pallas_call(
         finish,
         out_shape=(
             jax.ShapeDtypeStruct(inputs.shape, F32),
             jax.ShapeDtypeStruct(kernel.shape, F32),
-            jax.ShapeDtypeStruct((1, D), F32),
+            jax.ShapeDtypeStruct((D,), F32),
             jax.ShapeDtypeStruct(w_expand.shape, F32),
             jax.ShapeDtypeStruct(w_reduce.shape, F32),
-            jax.ShapeDtypeStruct(head_weight.shape, F32),
+            jax.ShapeDtypeStruct(head_rows.shape, F32),
         ),
         compiler_params=pltpu.CompilerParams(vmem_limit_bytes=32 * 1024 * 1024),
         name="finish",
-    )(o1, o2, direct)
-    return g_inputs, g_kernel, g_gain.reshape(D), g_expand, g_reduce, g_head
+    )(o1, o2, o3, direct)
+    return g_inputs, g_kernel, g_gain, g_expand, g_reduce, g_head.T
 
 
 def solution(mesh):

time: 99.5 us -> 82.6 us (0.83)
  local copies, waits for them, and re-layouts: 7.9 us -> 0 us
  Pallas kernels: 89.1 us -> 81.9 us
  other arithmetic: 1.45 us -> 0 us
    pallas_call x1, Pallas kernels: 86.3 us -> 79.2 us  [on_device(): pl.pallas_call(lambda *refs: work(sizes, *refs), out_shape=(jax.ShapeDtyp...]
    unnamed x10 -> x0, local copies, waits for them, and re-layouts: 6.13 us -> none
    reshape x2 -> x0, local copies, waits for them, and re-layouts: 1.68 us -> none  [the longest x1 0.99 us: on_device(): observed = target.reshape(outputs, 192)]
where the time goes in v2:
time: 82.6 us; the launch traced here: 82.5 us
  Pallas kernels  81.9 us (99%)
    pallas_call x1, Pallas kernels, on_device(): pl.pallas_call(lambda *refs: work(sizes, *refs), out_shape=(jax.ShapeDtyp...  79.2 us
    pallas_call x1, Pallas kernels, on_device(): pl.pallas_call(finish, out_shape=(jax.ShapeDtypeStruct(inputs.shape, F32)...  2.66 us

profile of v2, /device:TPU:1, one launch (start us, length us, event | category | flops | bytes accessed | tf_op | source)
XLA Modules:
  0.0 82.5 jit_solution(13828143588562344373)
XLA Ops:
  0.6 79.2 %block_pass.1 = (bf16[2,2560,128]{2,1,0:T(8,128)(2,1)S(1)}, bf16[2,2560,128]{2,1,0:T(8,128)(2,1)S(1)}, bf16[2,96,128]{2,1,0:T(8,128)(2,1)S(1)}, f32[2,12,16,384]{3,2,1,0:T(8,128)S(1)}) custom-call(bf16[2,12,16,384]{3,2,1,0:T(8,128)(2,1)} %refs_0_.1, f32[12,16,77]{2,1,0:T(8,128)} %bitcast.3, s32[12,16]{1,0:T(8,128)} %refs_2_.1, f32[7,7,384]{2,1,0:T(8,128)} %refs_3_.1, ...), custom_call_target="tpu_custom_call" | custom-call | tf_op jit(solution)/shard_map/block_pass/pallas_call | solution.py:872
  79.9 2.7 %finish.1 = (f32[2,12,16,384]{3,2,1,0:T(8,128)}, f32[7,7,384]{2,1,0:T(8,128)}, f32[384]{0:T(512)}, f32[384,1536]{1,0:T(8,128)}, f32[1536,384]{1,0:T(8,128)}, /*index=5*/f32[77,384]{1,0:T(8,128)}) custom-call(bf16[2,2560,128]{2,1,0:T(8,128)(2,1)S(1)} %get-tuple-element.16.o1, bf16[2,2560,128]{2,1,0:T(8,128)(2,1)S(1)} %get-tuple-element.17.o2, ...), custom_call_target="tpu_custom_call" | custom-call | tf_op jit(solution)/shard_map/finish/pallas_call | solution.py:888

commit v3 on v2

v3 whole, which is shorter than its diff:
```python
import jax
import jax.numpy as jnp
from jax import lax
from jax.experimental import pallas as pl
from jax.experimental.pallas import tpu as pltpu
from jax.sharding import PartitionSpec as P

FAIR_WEIGHT = 0.95
SMOOTHING = 0.5
NORM_EPS = 1e-06
D = 384
FFN = 1536
LANES = 3
BLOCK = 512
BLOCKS = FFN // BLOCK
MEMBERS = 8
HALF = 2048
SHARD = 64
MAIN = 48
SLOTS = 48
THIRD = 1024
COUNT_BITS = 8
FEW = 128
F32 = jnp.float32
BF16 = jnp.bfloat16


def grid_of(mesh):
    tiles = mesh.shape["tile"]
    side = 4 if tiles == 64 else 2
    return side, side, tiles // (side * side)


def dot(a, b, dims):
    return lax.dot_general(a, b, (dims, ((), ())), preferred_element_type=F32)


NN = ((1,), (0,))
NT = ((1,), (1,))
TN = ((0,), (0,))


class Place:
    def __init__(self, sizes):
        self.nx, self.ny, self.nzh = sizes
        self.nz = 2 * self.nzh
        self.tiles = self.nx * self.ny * self.nzh
        self.ens = lax.axis_index("ens")
        self.tile = lax.axis_index("tile")
        self.core = lax.rem(self.ens, 2)
        self.zl = lax.div(self.ens, 2)
        self.zh = lax.rem(self.tile, self.nzh)
        self.x = lax.rem(lax.div(self.tile, self.nzh), self.nx)
        self.y = lax.div(self.tile, self.nzh * self.nx)
        self.z = self.zh * 2 + self.zl

    def at(self, x, y, z, core):
        return (lax.rem(z, 2) * 2 + core, (y * self.nx + x) * self.nzh + lax.div(z, 2))

    def along_x(self, d):
        return self.at(lax.rem(self.x + d, self.nx), self.y, self.z, self.core)

    def along_y(self, d):
        return self.at(self.x, lax.rem(self.y + d, self.ny), self.z, self.core)

    def along_z(self, d):
        return self.at(self.x, self.y, lax.rem(self.z + d, self.nz), self.core)

    def other_core(self):
        return self.at(self.x, self.y, self.z, 1 - self.core)

    def along_tile(self, d):
        return (self.ens, lax.rem(self.tile + d + self.tiles, self.tiles))

    def along_ens(self, d):
        return (lax.rem(self.ens + d, 4), self.tile)

    def everyone(self):
        peers = [self.along_tile(1), self.along_tile(-1)]
        peers += [self.along_ens(d) for d in range(1, 4)]
        peers += [self.along_x(d) for d in range(1, self.nx)]
        peers += [self.along_y(d) for d in range(1, self.ny)]
        peers += [self.along_z(d) for d in range(1, self.nz)]
        return peers


def remote(src, dst, send, recv, to):
    return pltpu.make_async_remote_copy(
        src_ref=src,
        dst_ref=dst,
        send_sem=send,
        recv_sem=recv,
        device_id=to,
        device_id_type=pl.DeviceIdType.MESH,
    )


def far_first(size):
    return sorted(range(1, size), key=lambda d: -min(d, size - d))


def summed(parts):
    value = None
    for part in parts:
        part = part.astype(F32)
        value = part if value is None else value + part
    return value.astype(BF16)


def from_row(start, count):
    return pl.ds(pl.multiple_of(start, 16), count)


class Group:
    def __init__(self, owner, whole, apart=False):
        self.owner, self.whole, self.apart = owner, whole, apart
        self.send, self.recv = owner.send.at[owner.slot()], owner.recv.at[owner.slot()]
        self.copies = []
        owner.groups.append(self)

    def start(self, src, dst, to):
        recv = self.owner.recv.at[self.owner.slot()] if self.apart else self.recv
        copy = remote(src, dst, self.send, recv, to)
        copy.start()
        self.copies.append(copy)
        self.to = to

    def all(self):
        return remote(self.whole, self.whole, self.send, self.recv, self.to)

    def received(self):
        self.all().wait_recv()

    def sent(self):
        self.all().wait_send()


class Copies:
    def __init__(self, send, recv):
        self.send, self.recv = send, recv
        self.slots = 0
        self.groups = []

    def slot(self):
        self.slots += 1
        return self.slots - 1

    def one(self, src, dst, to):
        group = Group(self, src)
        group.start(src, dst, to)
        return group

    def keep(self, src, dst):
        copy = pltpu.make_async_copy(src, dst, self.send.at[self.slot()])
        copy.start()
        return copy

    def settle(self):
        for group in self.groups:
            group.sent()
        self.groups = []


class Reduce(Copies):
    def __init__(self, place, refs, out, third):
        self.third = third
        self.p = place
        self.g, self.rc, self.s1, self.r1, self.s2, self.r2, self.sz, self.rz, self.oz, *sems = refs
        super().__init__(*sems)
        self.out = out
        self.n, self.nz = place.nx, place.nz
        self.c_rows = HALF // 2
        self.p_rows = self.c_rows // self.n
        self.q_rows = self.p_rows // self.n
        self.z_rows = 2 * self.q_rows // self.nz
        self.order, self.z_order = far_first(self.n), far_first(self.nz)
        self.core = [None, None]
        self.in_first = [None, None]

    def first(self, h):
        return self.p.x if h == 0 else self.p.y

    def second(self, h):
        return self.p.y if h == 0 else self.p.x

    def to_first(self, h, d):
        return self.p.along_x(d) if h == 0 else self.p.along_y(d)

    def to_second(self, h, d):
        return self.p.along_y(d) if h == 0 else self.p.along_x(d)

    def start_core(self, halves=(0, 1)):
        other = from_row((1 - self.p.core) * self.c_rows, self.c_rows)
        for h in halves:
            self.core[h] = self.one(self.g.at[h, other], self.rc.at[h], self.p.other_core())

    def core_to_first(self, halves=(0, 1)):
        for h in halves:
            self.core[h].received()
            group = self.in_first[h] = Group(self, self.r1.at[h])
            for d in (*self.order, 0):
                at = lax.rem(self.first(h) + d, self.n) * self.p_rows
                piece = from_row(at, self.p_rows)
                mine = from_row(self.p.core * self.c_rows + at, self.p_rows)
                self.s1[h, piece, :] = summed([self.g[h, mine, :], self.rc[h, piece, :]])
                if d:
                    group.start(self.s1.at[h, piece], self.r1.at[h, d - 1], self.to_first(h, d))

    def first_to_second(self):
        self.in_second = []
        for h in range(2):
            self.in_first[h].received()
            mine = self.s1[h, from_row(self.first(h) * self.p_rows, self.p_rows), :]
            self.s2[h] = summed([mine, *(self.r1[h, d] for d in range(self.n - 1))])
            group = Group(self, self.r2.at[h])
            self.in_second.append(group)
            for d in self.order:
                piece = from_row(lax.rem(self.second(h) + d, self.n) * self.q_rows, self.q_rows)
                group.start(self.s2.at[h, piece], self.r2.at[h, d - 1], self.to_second(h, d))

    def second_to_z(self):
        for h in range(2):
            self.in_second[h].received()
            mine = self.s2[h, from_row(self.second(h) * self.q_rows, self.q_rows), :]
            self.sz[h * self.q_rows : (h + 1) * self.q_rows, :] = summed(
                [mine, *(self.r2[h, d] for d in range(self.n - 1))]
            )
        self.in_z = Group(self, self.rz)
        for d in self.z_order:
            piece = from_row(lax.rem(self.p.z + d, self.nz) * self.z_rows, self.z_rows)
            self.in_z.start(self.sz.at[piece], self.rz.at[d - 1], self.p.along_z(d))

    def z_to_gather(self):
        self.in_z.received()
        mine = from_row(self.p.z * self.z_rows, self.z_rows)
        self.oz[mine, :] = summed([self.sz[mine, :], *(self.rz[d] for d in range(self.nz - 1))])
        self.out_z = Group(self, self.oz.at[pl.ds(0, (self.nz - 1) * self.z_rows)])
        for d in self.z_order:
            self.out_z.start(self.oz.at[mine], self.oz.at[mine], self.p.along_z(d))

    def shard(self, h):
        return self.p.core * self.c_rows + self.first(h) * self.p_rows + self.second(h) * self.q_rows

    def gather_to_second(self):
        self.out_z.received()
        self.out_second = []
        self.kept = []
        for h in range(2):
            at = from_row(self.shard(h), self.q_rows)
            mine = self.oz.at[pl.ds(h * self.q_rows, self.q_rows)]
            group = Group(self, self.out.at[h, pl.ds(0, (self.n - 1) * self.q_rows)])
            self.out_second.append(group)
            for d in self.order:
                group.start(mine, self.out.at[h, at], self.to_second(h, d))
            self.kept.append(self.keep(mine, self.out.at[h, at]))

    def piece(self, h, d):
        at = lax.rem(self.first(h) + d, self.n) * self.p_rows
        return self.out.at[h, from_row(self.p.core * self.c_rows + at, self.p_rows)]

    def second_to_first(self):
        self.out_first = []
        self.out_core = []
        for h in range(2):
            self.out_second[h].received()
            self.kept[h].wait()
            mine = self.piece(h, 0)
            group = Group(self, self.out.at[h, pl.ds(0, (self.n - 1) * self.p_rows)], apart=True)
            self.out_first.append(group)
            for d in self.order:
                group.start(mine, mine, self.to_first(h, d))
            group = Group(self, self.out.at[h, pl.ds(0, self.c_rows)])
            self.out_core.append(group)
            group.start(mine, mine, self.p.other_core())

    def first_to_core(self):
        for k, d in enumerate(self.order):
            for h in range(2):
                self.out_first[h].copies[k].wait_recv()
                came = self.piece(h, self.n - d)
                self.out_core[h].start(came, came, self.p.other_core())

    def finish(self):
        for group in self.out_core:
            group.received()
        self.settle()


class Few(Copies):
    def __init__(self, place, refs, out):
        self.p = p = place
        self.g, self.rc, self.s, self.rx, self.sy, self.sz, self.o, *sems = refs
        super().__init__(*sems)
        self.out = out
        self.x_rows = FEW // p.nx

    def piece(self, d):
        return from_row(lax.rem(self.p.x + d, self.p.nx) * self.x_rows, self.x_rows)

    def start(self):
        self.got = self.one(self.g.at[1 - self.p.core], self.rc, self.p.other_core())

    def to_x(self):
        p = self.p
        self.got.received()
        self.s[...] = summed([self.g[p.core], self.rc[...]])
        self.got = Group(self, self.rx)
        for d in far_first(p.nx):
            self.got.start(self.s.at[self.piece(d)], self.rx.at[d - 1], p.along_x(d))

    def to_y(self):
        p = self.p
        self.got.received()
        self.sy[p.y] = summed([self.s[self.piece(0), :], *(self.rx[d] for d in range(p.nx - 1))])
        self.got = Group(self, self.sy.at[pl.ds(0, p.ny - 1)])
        for d in far_first(p.ny):
            self.got.start(self.sy.at[p.y], self.sy.at[p.y], p.along_y(d))

    def to_z(self):
        p = self.p
        self.got.received()
        self.sz[p.z] = summed(self.sy[k] for k in range(p.ny))
        self.got = Group(self, self.sz.at[pl.ds(0, p.nz - 1)])
        for d in far_first(p.nz):
            self.got.start(self.sz.at[p.z], self.sz.at[p.z], p.along_z(d))

    def to_gather(self):
        p = self.p
        self.got.received()
        self.o[...] = summed(self.sz[k] for k in range(p.nz))
        mine = self.out.at[p.core, self.piece(0)]
        self.kept = self.keep(self.o, mine)
        self.got = Group(self, self.out.at[0, pl.ds(0, (p.nx - 1) * self.x_rows)])
        for d in far_first(p.nx):
            self.got.start(self.o, mine, p.along_x(d))
        self.last = Group(self, self.out.at[0])
        self.last.start(self.o, mine, p.other_core())

    def to_core(self):
        p = self.p
        self.got.received()
        for d in range(1, p.nx):
            came = self.out.at[p.core, self.piece(d)]
            self.last.start(came, came, p.other_core())

    def finish(self):
        self.last.received()
        self.kept.wait()
        self.settle()


class Third(Copies):
    def __init__(self, place, refs, out):
        self.p = p = place
        self.g, self.rc, self.s1, self.r1, self.s2, self.r2, self.sy, self.o, *sems = refs
        super().__init__(*sems)
        self.out = out
        self.z_rows = THIRD // 2 // p.nz
        self.x_rows = self.z_rows // p.nx
        self.order = far_first(p.nz)

    def piece(self, d):
        return from_row(lax.rem(self.p.z + d, self.p.nz) * self.z_rows, self.z_rows)

    def start_core(self):
        self.got = self.one(self.g.at[1 - self.p.core], self.rc, self.p.other_core())

    def core_to_first(self):
        p = self.p
        self.got.received()
        self.s1[...] = summed([self.g[p.core], self.rc[...]])
        self.got = Group(self, self.r1)
        for d in self.order:
            self.got.start(self.s1.at[self.piece(d)], self.r1.at[d - 1], p.along_z(d))

    def first_to_second(self):
        p = self.p
        self.got.received()
        self.s2[...] = summed([self.s1[self.piece(0), :], *(self.r1[k] for k in range(p.nz - 1))])
        self.got = Group(self, self.r2)
        for d in far_first(p.nx):
            piece = from_row(lax.rem(p.x + d, p.nx) * self.x_rows, self.x_rows)
            self.got.start(self.s2.at[piece], self.r2.at[d - 1], p.along_x(d))

    def second_to_y(self):
        p = self.p
        self.got.received()
        mine = self.s2[from_row(p.x * self.x_rows, self.x_rows), :]
        self.sy[p.y] = summed([mine, *(self.r2[d] for d in range(p.nx - 1))])
        self.got = Group(self, self.sy.at[pl.ds(0, p.ny - 1)])
        for d in far_first(p.ny):
            self.got.start(self.sy.at[p.y], self.sy.at[p.y], p.along_y(d))

    def y_to_second(self):
        p = self.p
        self.got.received()
        self.o[...] = summed(self.sy[k] for k in range(p.ny))
        mine = self.out.at[p.core, from_row(p.z * self.z_rows + p.x * self.x_rows, self.x_rows)]
        self.kept = self.keep(self.o, mine)
        self.got = Group(self, self.out.at[0, pl.ds(0, (p.nx - 1) * self.x_rows)])
        for d in far_first(p.nx):
            self.got.start(self.o, mine, p.along_x(d))

    def second_to_first(self):
        p = self.p
        self.got.received()
        self.kept.wait()
        mine = self.out.at[p.core, self.piece(0)]
        self.got = Group(self, self.out.at[0, pl.ds(0, (p.nz - 1) * self.z_rows)])
        for d in self.order:
            self.got.start(mine, mine, p.along_z(d))

    def first_to_core(self):
        p = self.p
        self.got.received()
        self.last = self.one(self.out.at[p.core], self.out.at[p.core], p.other_core())

    def finish(self):
        self.last.received()
        self.settle()


def third_scratch(sizes):
    nx, ny, nzh = sizes
    nz = 2 * nzh
    z_rows = THIRD // 2 // nz
    x_rows = z_rows // nx
    shapes = [
        (2, THIRD // 2, 128), (THIRD // 2, 128), (THIRD // 2, 128), (nz - 1, z_rows, 128), (z_rows, 128),
        (nx - 1, x_rows, 128), (ny, x_rows, 128), (x_rows, 128),
    ]
    return [pltpu.VMEM(shape, BF16) for shape in shapes] + [pltpu.SemaphoreType.DMA((SLOTS,))] * 2


def few_scratch(sizes):
    nx, ny, nzh = sizes
    x_rows = FEW // nx
    shapes = [
        (2, FEW, 128), (FEW, 128), (FEW, 128), (nx - 1, x_rows, 128), (ny, x_rows, 128), (2 * nzh, x_rows, 128),
        (x_rows, 128),
    ]
    return [pltpu.VMEM(shape, BF16) for shape in shapes] + [pltpu.SemaphoreType.DMA((SLOTS,))] * 2


def reduce_scratch(sizes):
    n, _, nzh = sizes
    nz = 2 * nzh
    c_rows = HALF // 2
    p_rows = c_rows // n
    q_rows = p_rows // n
    z_rows = 2 * q_rows // nz
    shapes = [
        (2, HALF, 128), (2, c_rows, 128), (2, c_rows, 128), (2, n - 1, p_rows, 128), (2, p_rows, 128),
        (2, n - 1, q_rows, 128), (2 * q_rows, 128), (nz - 1, z_rows, 128), (2 * q_rows, 128),
    ]
    return [pltpu.VMEM(shape, BF16) for shape in shapes] + [pltpu.SemaphoreType.DMA((SLOTS,))] * 2


def slope_of(offset):
    return offset * lax.rsqrt(offset * offset + SMOOTHING * SMOOTHING)


def places(flat, count):
    at = 0
    while at < count:
        here = flat + at
        if here < HALF:
            take, part, row = HALF - here, 0, here
        elif here < HALF + 32 * MAIN:
            shard, inner = divmod(here - HALF, MAIN)
            take, part, row = MAIN - inner, 1, shard * SHARD + inner
        else:
            row = here - HALF - 32 * MAIN
            part, row = 2 + row // (THIRD // 2), row % (THIRD // 2)
            take = THIRD // 2 - row
        take = min(take, count - at)
        yield at, part, row, take
        at += take


def part_of(halves, third, part):
    return halves.at[part] if part < 2 else third.at[part - 2]


def put_main(batch, flat, value):
    for at, part, row, take in places(flat, value.shape[0]):
        part_of(batch.g, batch.third.g, part)[row : row + take, :] = value[at : at + take].astype(BF16)


def put_small(batch, index, value):
    batch[1, index * SHARD + MAIN : (index + 1) * SHARD, :] = value.astype(BF16)


def put_few(batch, index, value):
    batch[index // 6, index % 6 * 16 : index % 6 * 16 + 16, :] = value.astype(BF16)


def work(sizes, *refs):
    (
        x_hbm, target_hbm, sea_hbm, kernel_hbm, gain_hbm, expand_hbm, reduce_hbm, head_hbm,
        out1, third1, out2, third2, out3, direct_out,
        xb, target, tall, tg, sea, taps, gain, we, wr, head,
        ext, dext, rim, hs, hr, hs2, hr2, mixed, standard, recip, normed, before, slope, hidden, hidden_t, normed_t,
        block, head_t, fall, d_block, d_block_b, d_before, d_norm, gk,
        in_sems, halo_send, halo_recv, ens_send, ens_recv,
        *rest,
    ) = refs
    place = Place(sizes)
    few = Few(place, rest[-9:], out3)
    pieces = (len(rest) - 9) // 2
    batch1, batch2 = (
        Reduce(place, mine[:-10], out, Third(place, mine[-10:], third))
        for mine, out, third in ((rest[:pieces], out1, third1), (rest[pieces : 2 * pieces], out2, third2))
    )

    loads = [
        pltpu.make_async_copy(x_hbm.at[0, 0:8], xb.at[0:8], in_sems.at[0]),
        pltpu.make_async_copy(x_hbm.at[1, 0:8], xb.at[8:16], in_sems.at[1]),
        pltpu.make_async_copy(x_hbm.at[0, 8:12], xb.at[16:20], in_sems.at[2]),
        pltpu.make_async_copy(x_hbm.at[1, 8:12], xb.at[20:24], in_sems.at[3]),
    ]
    tap_loads = [
        pltpu.make_async_copy(kernel_hbm.at[:, :, l * 128 : (l + 1) * 128], taps.at[l], in_sems.at[4 + l])
        for l in range(LANES)
    ]
    later = [
        pltpu.make_async_copy(gain_hbm, gain, in_sems.at[7]),
        pltpu.make_async_copy(head_hbm, head, in_sems.at[8]),
        pltpu.make_async_copy(expand_hbm, we, in_sems.at[9]),
        pltpu.make_async_copy(reduce_hbm, wr, in_sems.at[10]),
        pltpu.make_async_copy(target_hbm, target, in_sems.at[11]),
        pltpu.make_async_copy(sea_hbm, sea, in_sems.at[12]),
    ]
    for copy in loads + tap_loads + later:
        copy.start()

    barrier = pltpu.get_barrier_semaphore()
    peers = place.everyone()
    for peer in peers:
        pl.semaphore_signal(barrier, inc=1, device_id=peer, device_id_type=pl.DeviceIdType.MESH)

    def clear(i, _):
        l, m = lax.div(i, 2), lax.rem(i, 2)
        for ref in (ext, dext):
            ref[l, m, 0:3] = jnp.zeros((3, 32, 128), F32)
            ref[l, m, 15:18] = jnp.zeros((3, 32, 128), F32)
        ext[l, m, 3:15, 0:8] = jnp.zeros((12, 8, 128), F32)
        ext[l, m, 3:15, 24:32] = jnp.zeros((12, 8, 128), F32)
        return 0

    lax.fori_loop(0, 2 * LANES, clear, 0)
    gk[...] = jnp.zeros_like(gk)
    rim[...] = jnp.zeros_like(rim)
    few.g[...] = jnp.zeros_like(few.g)
    for copy in loads:
        copy.wait()
    for l in range(LANES):
        lanes = slice(l * 128, (l + 1) * 128)
        for m in range(2):
            ext[l, m, 3:11, 8:24, :] = xb[m * 8 : m * 8 + 8, :, lanes].astype(F32)
            ext[l, m, 11:15, 8:24, :] = xb[16 + m * 4 : 20 + m * 4, :, lanes].astype(F32)

    def rim_rows(m, j):
        return slice((m * 3 + j) * 12, (m * 3 + j) * 12 + 12)

    def pack(field, out):
        for side, col in ((0, 8), (1, 21)):
            for m in range(2):
                for j in range(3):
                    for l in range(LANES):
                        rim[side, l, rim_rows(m, j)] = field[l, m, 3:15, col + j, :]
        out[...] = rim[...].astype(BF16)

    def unpack(field, got, l):
        for side, col in ((0, 5), (1, 24)):
            rim[side, l] = got[side, l].astype(F32)
            for m in range(2):
                for j in range(3):
                    field[l, m, 3:15, col + j, :] = rim[side, l, rim_rows(m, j)]

    def halo(out, got, at):
        copies = [
            [
                remote(out.at[side, l], got.at[1 - side, l], halo_send.at[at + s], halo_recv.at[at + s], place.along_tile(to))
                for s, (side, to) in enumerate(((0, -1), (1, 1)), 2 * l)
            ]
            for l in range(LANES)
        ]
        for pair in copies:
            for copy in pair:
                copy.start()
        return copies

    pack(ext, hs)
    pl.semaphore_wait(barrier, len(peers))
    halo1 = halo(hs, hr, 0)

    for copy in tap_loads + later:
        copy.wait()
    for index in range(32):
        put_small(batch1.g, index, jnp.zeros((16, 128), F32))
        if index >= 15:
            put_small(batch2.g, index, jnp.zeros((16, 128), F32))
    outputs = head.shape[0]
    head_t[...] = jnp.concatenate([head[...].astype(F32), jnp.zeros((80 - outputs, D), F32)], axis=0).astype(BF16)
    diagonal = lax.broadcasted_iota(jnp.int32, (16, 16), 0) == lax.broadcasted_iota(jnp.int32, (16, 16), 1)
    tall[...] = jnp.zeros_like(tall)
    for a in range(12):
        water = jnp.broadcast_to(sea[a : a + 1, :].astype(F32), (16, 16))
        water = jnp.sum(jnp.where(diagonal, water, 0.0), axis=1, keepdims=True)
        for at in (a * 16,) if a < 8 else (a * 16, a * 16 + 64):
            tall[at : at + 16, 0:outputs] = target[a]
            tall[at : at + 16, outputs : outputs + 1] = water
    tg[...] = tall[...].T[0:80]
    def correlate(field, l, m, flip):
        total = jnp.zeros((12, 16, 128), F32)
        for j in range(7):
            shifted = field[l, m, :, 5 + j : 21 + j, :]
            for i in range(7):
                tap = taps[l, 6 - i, 6 - j : 7 - j, :] if flip else taps[l, i, j : j + 1, :]
                total = total + shifted[i : i + 12] * tap
        return total

    def mix(i, _):
        l, m = lax.div(i, 2), lax.rem(i, 2)
        total = correlate(ext, l, m, False)
        mixed[l, pl.ds(m * 8, 8)] = total[:8]
        mixed[l, pl.ds(16 + m * 4, 4)] = total[8:]
        return 0

    lax.fori_loop(0, 2 * LANES, mix, 0)
    sublane = lax.broadcasted_iota(jnp.int32, (18, 8, 128), 1)

    def edges(l, m):
        for first, taps_in in ((0, (0, 1, 2)), (8, (4, 5, 6))):
            total = jnp.zeros((12, 8, 128), F32)
            for j in taps_in:
                outside = sublane < 3 - j if first == 0 else sublane >= 11 - j
                shifted = jnp.where(outside, ext[l, m, :, 5 + first + j : 13 + first + j, :], 0.0)
                for i in range(7):
                    total = total + shifted[i : i + 12] * taps[l, i, j : j + 1, :]
            mixed[l, pl.ds(m * 8, 8), first : first + 8] += total[:8]
            mixed[l, pl.ds(16 + m * 4, 4), first : first + 8] += total[8:]

    for l in range(LANES):
        for copy in halo1[l]:
            copy.wait_recv()
        unpack(ext, hr, l)
        lax.fori_loop(0, 2, lambda m, _, l=l: (edges(l, m), 0)[1], 0)

    gain_row = gain[...].reshape(1, D)

    def norm(i, _):
        rows = pl.ds(pl.multiple_of(i * 64, 64), 64)
        parts = [mixed[l, pl.ds(i * 4, 4)].reshape(64, 128) for l in range(LANES)]
        mean = jnp.sum(parts[0] + parts[1] + parts[2], axis=-1, keepdims=True) / D
        centre = [part - mean for part in parts]
        square = centre[0] * centre[0] + centre[1] * centre[1] + centre[2] * centre[2]
        scale = lax.rsqrt(jnp.sum(square, axis=-1, keepdims=True) / D + NORM_EPS)
        recip[rows, :] = jnp.broadcast_to(scale, (64, 128))
        for l in range(LANES):
            lanes = slice(l * 128, (l + 1) * 128)
            value = centre[l] * scale
            standard[rows, lanes] = value
            normed[rows, lanes] = (value * gain_row[:, lanes]).astype(BF16)
        return 0

    lax.fori_loop(0, 6, norm, 0)

    total = xb[...].reshape(D, D).astype(F32)
    for b in range(BLOCKS):
        columns = slice(b * BLOCK, (b + 1) * BLOCK)
        before[...] = dot(normed[...], we[:, columns], NN)

        def gelu(i, _):
            rows = pl.ds(pl.multiple_of(i * 32, 32), 32)
            v = before[rows, :]
            square = v * v
            scale = 0.7978845608028654
            t = jnp.tanh(v * (scale + (scale * 0.044715) * square))
            half = 0.5 + 0.5 * t
            hidden[rows, columns] = (v * half).astype(BF16)
            slope[rows, columns] = half + (0.5 * v) * (1.0 - t * t) * (scale + (scale * 3 * 0.044715) * square)
            return 0

        lax.fori_loop(0, 12, gelu, 0)
        total = total + dot(hidden[:, columns], wr[columns, :], NN)
    block[...] = total.astype(BF16)

    own = dot(head_t[...], block[...], NT)
    fall[0] = own
    far = place.along_ens(2)
    far_copies = [
        remote(fall.at[0, pl.ds(r, 40)], fall.at[2, pl.ds(r, 40)], ens_send.at[k], ens_recv.at[k], far)
        for k, r in enumerate((0, 40))
    ]
    near_copy = remote(fall.at[0], fall.at[1], ens_send.at[2], ens_recv.at[2], place.other_core())
    relays = [
        remote(fall.at[2, pl.ds(r, 40)], fall.at[3, pl.ds(r, 40)], ens_send.at[3 + k], ens_recv.at[3 + k], place.other_core())
        for k, r in enumerate((0, 40))
    ]
    for copy in [*far_copies, near_copy]:
        copy.start()
    normed_t[...] = normed[...].T
    for b in range(BLOCKS):
        hidden_t[b * BLOCK : (b + 1) * BLOCK, :] = hidden[:, b * BLOCK : (b + 1) * BLOCK].T
    for came, relay in zip(far_copies, relays):
        came.wait_recv()
        relay.start()
    near_copy.wait_recv()

    spread = jnp.zeros((80, D), F32)
    for s in range(4):
        if s == 3:
            for copy in relays:
                copy.wait_recv()
        theirs = fall[s]
        swapped = jnp.concatenate(
            [theirs[:, 128:256], theirs[:, 0:128], pltpu.roll(theirs[:, 256:384], 64, 1)], axis=1
        )
        spread = spread + slope_of(own - theirs) + slope_of(own - swapped)
    observed = jnp.concatenate([tg[:, 0:128], tg[:, 0:128], tg[:, 128:256]], axis=1)
    ocean = observed[outputs : outputs + 1]
    slopes = slope_of(own - observed) / MEMBERS - FAIR_WEIGHT / (MEMBERS * (MEMBERS - 1)) * spread
    slopes_b = (slopes * ocean).astype(BF16)

    back = dot(slopes_b, head_t[...], TN)
    d_block[...] = back
    d_block_b[...] = back.astype(BF16)
    grad_reduce = dot(hidden_t[...], d_block_b[...], NN)
    for l in range(LANES):
        put_main(batch1, l * FFN, grad_reduce[:, l * 128 : (l + 1) * 128])
    batch1.start_core()
    batch1.third.start_core()

    grad_head = dot(slopes_b, block[...], NN)
    for r in range(5):
        for l in range(LANES):
            put_small(batch2.g, r * 3 + l, grad_head[r * 16 : r * 16 + 16, l * 128 : (l + 1) * 128])

    d_normed = jnp.zeros((D, D), F32)
    for b in range(BLOCKS):
        columns = slice(b * BLOCK, (b + 1) * BLOCK)
        before[...] = dot(d_block_b[...], wr[columns, :], NT)

        def gate(i, _):
            rows = pl.ds(pl.multiple_of(i * 32, 32), 32)
            d_before[rows, :] = (before[rows, :] * slope[rows, columns]).astype(BF16)
            return 0

        lax.fori_loop(0, 12, gate, 0)
        grad_expand = dot(normed_t[...], d_before[...], NN)
        for l in range(BLOCK // 128):
            put_main(batch2, (b * (BLOCK // 128) + l) * D, grad_expand[:, l * 128 : (l + 1) * 128])
        d_normed = d_normed + dot(d_before[...], we[:, columns], NT)
        if b == 1:
            batch2.start_core((0,))
            batch1.core_to_first()
            batch1.third.core_to_first()
    batch2.start_core((1,))
    batch2.third.start_core()
    batch2.core_to_first((0,))
    d_norm[...] = d_normed

    gk[0, 7:8, :] = jnp.zeros((1, 128), F32)

    def unnorm(i, _):
        rows = pl.ds(pl.multiple_of(i * 64, 64), 64)
        value = [d_norm[rows, l * 128 : (l + 1) * 128] for l in range(LANES)]
        std = [standard[rows, l * 128 : (l + 1) * 128] for l in range(LANES)]
        for l in range(LANES):
            gk[l, 7:8, :] += jnp.sum(value[l] * std[l], axis=0, keepdims=True)
        scaled = [value[l] * gain_row[:, l * 128 : (l + 1) * 128] for l in range(LANES)]
        mean = jnp.sum(scaled[0] + scaled[1] + scaled[2], axis=-1, keepdims=True) / D
        along = jnp.sum(scaled[0] * std[0] + scaled[1] * std[1] + scaled[2] * std[2], axis=-1, keepdims=True) / D
        for l in range(LANES):
            mixed[l, pl.ds(i * 4, 4)] = (recip[rows, :] * (scaled[l] - mean - std[l] * along)).reshape(4, 16, 128)
        return 0

    lax.fori_loop(0, 6, unnorm, 0)
    for l in range(LANES):
        for m in range(2):
            dext[l, m, 3:11, 8:24, :] = mixed[l, m * 8 : m * 8 + 8]
            dext[l, m, 11:15, 8:24, :] = mixed[l, 16 + m * 4 : 20 + m * 4]
    pack(dext, hs2)
    halo2 = halo(hs2, hr2, 6)

    def kernel_grad(l, _):
        for j in range(7):
            near = [ext[l, m, :, 5 + j : 21 + j, :] for m in range(2)]
            for i in range(7):
                part = jnp.zeros((16, 128), F32)
                for m in range(2):
                    part = part + jnp.sum(dext[l, m, 3:15, 8:24, :] * near[m][i : i + 12], axis=0)
                gk[l, i * 8 + j : i * 8 + j + 1, :] = jnp.sum(part, axis=0, keepdims=True)
        return 0

    lax.fori_loop(0, 1, kernel_grad, 0)
    batch2.core_to_first((1,))
    batch2.third.core_to_first()
    lax.fori_loop(1, 3, kernel_grad, 0)
    count = jnp.sum(sea[...].astype(F32)).astype(jnp.int32)
    lane = lax.broadcasted_iota(jnp.int32, (1, 128), 1)
    bits = lax.bitwise_and(lax.shift_right_logical(jnp.broadcast_to(count, (1, 128)), jnp.minimum(lane, 31)), 1)
    gk[0, 15:16, :] = jnp.where(lane < COUNT_BITS, bits, 0).astype(F32)
    for r in range(4):
        for l in range(LANES):
            put_few(few.g, r * 3 + l, gk[l, r * 16 : r * 16 + 16, :])
    few.start()
    batch1.first_to_second()
    batch1.third.first_to_second()
    few.to_x()
    for l in range(LANES):
        for copy in halo2[l]:
            copy.wait_recv()
        unpack(dext, hr2, l)

    def mix_back(i, _):
        l, m = lax.div(i, 2), lax.rem(i, 2)
        mixed_back = correlate(dext, l, m, True)
        mixed[l, pl.ds(m * 8, 8)] = mixed_back[:8]
        mixed[l, pl.ds(16 + m * 4, 4)] = mixed_back[8:]
        return 0

    lax.fori_loop(0, 2, mix_back, 0)
    batch1.second_to_z()
    batch1.third.second_to_y()
    lax.fori_loop(2, 4, mix_back, 0)
    batch2.first_to_second()
    batch2.third.first_to_second()
    few.to_y()
    lax.fori_loop(4, 6, mix_back, 0)
    for l in range(LANES):
        lanes = slice(l * 128, (l + 1) * 128)
        mixed[l] = mixed[l] + d_block[:, lanes].reshape(24, 16, 128)
    direct = []
    for l in range(LANES):
        for m in range(2):
            lanes = slice(l * 128, (l + 1) * 128)
            at = (l * 2 + m) * 2
            direct.append(
                pltpu.make_async_copy(
                    mixed.at[l, m * 8 : m * 8 + 8], direct_out.at[m, 0:8, :, lanes], in_sems.at[at]
                )
            )
            direct.append(
                pltpu.make_async_copy(
                    mixed.at[l, 16 + m * 4 : 20 + m * 4], direct_out.at[m, 8:12, :, lanes], in_sems.at[at + 1]
                )
            )
    for copy in direct:
        copy.start()
    batch1.third.y_to_second()
    batch1.z_to_gather()
    batch2.second_to_z()
    batch2.third.second_to_y()
    few.to_z()
    batch1.third.second_to_first()
    batch1.gather_to_second()
    batch2.third.y_to_second()
    batch2.z_to_gather()
    for each in (few, batch1, batch1.third, batch2, batch2.third):
        each.settle()
    few.to_gather()
    batch1.second_to_first()
    batch2.third.second_to_first()
    batch2.gather_to_second()
    few.to_core()
    batch1.third.first_to_core()
    batch2.second_to_first()
    batch1.first_to_core()
    batch2.third.first_to_core()
    batch2.first_to_core()
    for copy in sum(halo1 + halo2, []) + far_copies + [near_copy] + relays:
        copy.wait_send()
    for copy in direct:
        copy.wait()
    few.finish()
    for batch in (batch1, batch2):
        batch.third.finish()
        batch.finish()


def finish(
    o1, t1, o2, t2, o3, direct, g_inputs, g_kernel, g_gain, g_expand, g_reduce, g_head, kernel, gain, expand, reduce, head, sems
):
    copies = []

    def write(src, dst):
        copy = pltpu.make_async_copy(src, dst, sems.at[len(copies)])
        copy.start()
        copies.append(copy)

    def few(index):
        return o3[index // 6, index % 6 * 16 : index % 6 * 16 + 16, :].astype(F32)

    write(direct, g_inputs)
    rows = [[few(r * 3 + l) for l in range(LANES)] for r in range(4)]
    weight = lax.broadcasted_iota(jnp.int32, (1, 128), 1)
    weight = jnp.where(weight < COUNT_BITS, lax.shift_left(1, jnp.minimum(weight, 15)), 0).astype(F32)
    total = jnp.sum(rows[0][0][15:16] * weight, axis=-1, keepdims=True) / 4
    scale = 1.0 / total

    def main(halves, third, flat, count):
        for at, part, row, take in places(flat, count):
            yield at, take, part_of(halves, third, part)[row : row + take, :].astype(F32) * scale

    for r in range(0, FFN, 512):
        for l in range(LANES):
            for at, take, part in main(o1, t1, l * FFN + r, 512):
                reduce[r + at : r + at + take, l * 128 : (l + 1) * 128] = part
        write(reduce.at[r : r + 512], g_reduce.at[r : r + 512])
    for r in range(0, D, 128):
        for l in range(FFN // 128):
            for at, take, part in main(o2, t2, l * D + r, 128):
                expand[r + at : r + at + take, l * 128 : (l + 1) * 128] = part
        write(expand.at[r : r + 128], g_expand.at[r : r + 128])
    for l in range(LANES):
        lanes = slice(l * 128, (l + 1) * 128)
        for i in range(7):
            at = (i % 2) * 8
            kernel[i, :, lanes] = rows[i // 2][l][at : at + 7] * scale
        gain[lanes] = (rows[0][l][7:8] * scale).reshape(128)
        for r in range(5):
            index = r * 3 + l
            part = o2[1, index * SHARD + MAIN : (index + 1) * SHARD, :].astype(F32) * scale
            count = min(16, head.shape[0] - r * 16)
            head[r * 16 : r * 16 + count, lanes] = part[:count]
    write(kernel, g_kernel)
    write(gain, g_gain)
    write(head, g_head)
    for copy in copies:
        copy.wait()


def on_device(sizes, inputs, target, land_sea, kernel, norm_gain, w_expand, w_reduce, head_weight):
    outputs = target.shape[0]
    by_cell = jnp.transpose(target, (1, 2, 0))
    head_rows = head_weight.T
    anywhere = pl.BlockSpec(memory_space=pl.ANY)
    in_hbm = pl.BlockSpec(memory_space=pltpu.HBM)
    vmem = pltpu.VMEM
    scratch = [
        vmem((24, 16, D), BF16),
        vmem((12, 16, outputs), F32),
        vmem((256, 128), F32),
        vmem((80, 256), F32),
        vmem((12, 16), jnp.int32),
        vmem((LANES, 7, 7, 128), F32),
        vmem((D,), F32),
        vmem((D, FFN), BF16),
        vmem((FFN, D), BF16),
        vmem((outputs, D), BF16),
        vmem((LANES, 2, 18, 32, 128), F32),
        vmem((LANES, 2, 18, 32, 128), F32),
        vmem((2, LANES, 80, 128), F32),
        vmem((2, LANES, 80, 128), BF16),
        vmem((2, LANES, 80, 128), BF16),
        vmem((2, LANES, 80, 128), BF16),
        vmem((2, LANES, 80, 128), BF16),
        vmem((LANES, 24, 16, 128), F32),
        vmem((D, D), F32),
        vmem((D, 128), F32),
        vmem((D, D), BF16),
        vmem((D, BLOCK), F32),
        vmem((D, FFN), F32),
        vmem((D, FFN), BF16),
        vmem((FFN, D), BF16),
        vmem((D, D), BF16),
        vmem((D, D), BF16),
        vmem((80, D), BF16),
        vmem((4, 80, D), F32),
        vmem((D, D), F32),
        vmem((D, D), BF16),
        vmem((D, BLOCK), BF16),
        vmem((D, D), F32),
        vmem((LANES, 64, 128), F32),
        pltpu.SemaphoreType.DMA((13,)),
        pltpu.SemaphoreType.DMA((12,)),
        pltpu.SemaphoreType.DMA((12,)),
        pltpu.SemaphoreType.DMA((5,)),
        pltpu.SemaphoreType.DMA((5,)),
    ]
    batch = reduce_scratch(sizes)
    batch = [*batch, *third_scratch(sizes)]
    scratch += batch + batch + few_scratch(sizes)
    operands = [inputs, by_cell, land_sea, kernel, norm_gain, w_expand, w_reduce, head_rows]
    operands = [pltpu.with_memory_space_constraint(operand, pltpu.HBM) for operand in operands]
    *reduced, direct = pl.pallas_call(
        lambda *refs: work(sizes, *refs),
        out_shape=(
            *(jax.ShapeDtypeStruct((2, rows, 128), BF16) for rows in (HALF, THIRD // 2, HALF, THIRD // 2, FEW)),
            jax.ShapeDtypeStruct(inputs.shape, F32),
        ),
        in_specs=[in_hbm] * 8,
        out_specs=(anywhere,) * 6,
        scratch_shapes=scratch,
        compiler_params=pltpu.CompilerParams(
            collective_id=0, has_side_effects=True, vmem_limit_bytes=48 * 1024 * 1024
        ),
        name="block_pass",
    )(*operands)
    in_vmem = pl.BlockSpec(memory_space=pltpu.VMEM)
    shapes = (kernel.shape, norm_gain.shape, w_expand.shape, w_reduce.shape, head_rows.shape)
    g_inputs, g_kernel, g_gain, g_expand, g_reduce, g_head = pl.pallas_call(
        finish,
        out_shape=tuple(jax.ShapeDtypeStruct(shape, F32) for shape in (inputs.shape, *shapes)),
        in_specs=[in_vmem] * 5 + [anywhere],
        out_specs=(anywhere,) * 6,
        scratch_shapes=[vmem(shape, F32) for shape in shapes] + [pltpu.SemaphoreType.DMA((11,))],
        compiler_params=pltpu.CompilerParams(vmem_limit_bytes=32 * 1024 * 1024),
        name="finish",
    )(*reduced, direct)
    return g_inputs, g_kernel, g_gain, g_expand, g_reduce, g_head.T


def solution(mesh):
    sizes = grid_of(mesh)
    return jax.shard_map(
        lambda *arrays: on_device(sizes, *arrays),
        mesh=mesh,
        in_specs=(
            P("ens", None, "tile", None),
            P(None, None, "tile"),
            P(None, "tile"),
            P(),
            P(),
            P(),
            P(),
            P(),
        ),
        out_specs=(P("ens", None, "tile", None), P(), P(), P(), P(), P()),
        check_vma=False,
    )
```

time: 82.6 us -> 77.9 us (0.943)
  Pallas kernels: 81.9 us -> 77.2 us
    pallas_call x2, Pallas kernels: 81.9 us -> 77.2 us  [the longest x1 74.7 us: on_device(): pl.pallas_call(lambda *refs: work(sizes, *refs), out_shape=(*(jax.ShapeDt...]
where the time goes in v3:
time: 77.9 us; the launch traced here: 77.8 us
  Pallas kernels  77.2 us (99%)
    pallas_call x1, Pallas kernels, on_device(): pl.pallas_call(lambda *refs: work(sizes, *refs), out_shape=(*(jax.ShapeDt...  74.7 us
    pallas_call x1, Pallas kernels, on_device(): pl.pallas_call(finish, out_shape=tuple((jax.ShapeDtypeStruct(shape, F32)...  2.5 us

profile of v3, /device:TPU:1, one launch (start us, length us, event | category | flops | bytes accessed | tf_op | source)
XLA Modules:
  0.0 77.8 jit_solution(3379209153137335776)
XLA Ops:
  0.6 74.7 %block_pass.1 = (bf16[2,2048,128]{2,1,0:T(8,128)(2,1)S(1)}, bf16[2,512,128]{2,1,0:T(8,128)(2,1)S(1)}, bf16[2,2048,128]{2,1,0:T(8,128)(2,1)S(1)}, bf16[2,512,128]...) custom-call(bf16[2,12,16,384]{3,2,1,0:T(8,128)(2,1)} %refs_0_.1, ...), custom_call_target="tpu_custom_call" | custom-call | tf_op jit(solution)/shard_map/block_pass/pallas_call | solution.py:989
  75.3 2.5 %finish.1 = (f32[2,12,16,384]{3,2,1,0:T(8,128)}, f32[7,7,384]{2,1,0:T(8,128)}, f32[384]{0:T(512)}, f32[384,1536]{1,0:T(8,128)}, f32[1536,384]{1,0:T(8,128)}, /*index=5*/f32[77,384]{1,0:T(8,128)}) custom-call(bf16[2,2048,128]{2,1,0:T(8,128)(2,1)S(1)} %get-tuple-element.18.o1, bf16[2,512,128]{2,1,0:T(8,128)(2,1)S(1)} %get-tuple-element.19.t1, ...), custom_call_target="tpu_custom_call" | custom-call | tf_op jit(solution)/shard_map/finish/pallas_call | solution.py:1005

commit v4 on v3

--- a/solution.py
+++ b/solution.py
@@ -176,6 +176,7 @@
         self.order, self.z_order = far_first(self.n), far_first(self.nz)
         self.core = [None, None]
         self.in_first = [None, None]
+        self.in_second = [None, None]
 
     def first(self, h):
         return self.p.x if h == 0 else self.p.y
@@ -206,14 +207,12 @@
                 if d:
                     group.start(self.s1.at[h, piece], self.r1.at[h, d - 1], self.to_first(h, d))
 
-    def first_to_second(self):
-        self.in_second = []
-        for h in range(2):
+    def first_to_second(self, halves=(0, 1)):
+        for h in halves:
             self.in_first[h].received()
             mine = self.s1[h, from_row(self.first(h) * self.p_rows, self.p_rows), :]
             self.s2[h] = summed([mine, *(self.r1[h, d] for d in range(self.n - 1))])
-            group = Group(self, self.r2.at[h])
-            self.in_second.append(group)
+            group = self.in_second[h] = Group(self, self.r2.at[h])
             for d in self.order:
                 piece = from_row(lax.rem(self.second(h) + d, self.n) * self.q_rows, self.q_rows)
                 group.start(self.s2.at[h, piece], self.r2.at[h, d - 1], self.to_second(h, d))
@@ -738,21 +737,19 @@
         for l in range(LANES):
             put_small(batch2.g, r * 3 + l, grad_head[r * 16 : r * 16 + 16, l * 128 : (l + 1) * 128])
 
-    d_normed = jnp.zeros((D, D), F32)
     for b in range(BLOCKS):
         columns = slice(b * BLOCK, (b + 1) * BLOCK)
         before[...] = dot(d_block_b[...], wr[columns, :], NT)
 
         def gate(i, _):
             rows = pl.ds(pl.multiple_of(i * 32, 32), 32)
-            d_before[rows, :] = (before[rows, :] * slope[rows, columns]).astype(BF16)
+            d_before[rows, columns] = (before[rows, :] * slope[rows, columns]).astype(BF16)
             return 0
 
         lax.fori_loop(0, 12, gate, 0)
-        grad_expand = dot(normed_t[...], d_before[...], NN)
+        grad_expand = dot(normed_t[...], d_before[:, columns], NN)
         for l in range(BLOCK // 128):
             put_main(batch2, (b * (BLOCK // 128) + l) * D, grad_expand[:, l * 128 : (l + 1) * 128])
-        d_normed = d_normed + dot(d_before[...], we[:, columns], NT)
         if b == 1:
             batch2.start_core((0,))
             batch1.core_to_first()
@@ -760,7 +757,9 @@
     batch2.start_core((1,))
     batch2.third.start_core()
     batch2.core_to_first((0,))
-    d_norm[...] = d_normed
+    d_norm[...] = dot(d_before[...], we[...], NT)
+    batch2.core_to_first((1,))
+    batch2.third.core_to_first()
 
     gk[0, 7:8, :] = jnp.zeros((1, 128), F32)
 
@@ -795,10 +794,15 @@
                 gk[l, i * 8 + j : i * 8 + j + 1, :] = jnp.sum(part, axis=0, keepdims=True)
         return 0
 
+    batch1.first_to_second()
+    batch2.first_to_second((0,))
     lax.fori_loop(0, 1, kernel_grad, 0)
-    batch2.core_to_first((1,))
-    batch2.third.core_to_first()
-    lax.fori_loop(1, 3, kernel_grad, 0)
+    batch1.third.first_to_second()
+    batch2.first_to_second((1,))
+    batch1.second_to_z()
+    lax.fori_loop(1, 2, kernel_grad, 0)
+    batch2.third.first_to_second()
+    lax.fori_loop(2, 3, kernel_grad, 0)
     count = jnp.sum(sea[...].astype(F32)).astype(jnp.int32)
     lane = lax.broadcasted_iota(jnp.int32, (1, 128), 1)
     bits = lax.bitwise_and(lax.shift_right_logical(jnp.broadcast_to(count, (1, 128)), jnp.minimum(lane, 31)), 1)
@@ -807,9 +811,8 @@
         for l in range(LANES):
             put_few(few.g, r * 3 + l, gk[l, r * 16 : r * 16 + 16, :])
     few.start()
-    batch1.first_to_second()
-    batch1.third.first_to_second()
-    few.to_x()
+    batch2.second_to_z()
+    batch1.third.second_to_y()
     for l in range(LANES):
         for copy in halo2[l]:
             copy.wait_recv()
@@ -823,12 +826,12 @@
         return 0
 
     lax.fori_loop(0, 2, mix_back, 0)
-    batch1.second_to_z()
-    batch1.third.second_to_y()
+    batch1.z_to_gather()
+    batch2.third.second_to_y()
+    few.to_x()
     lax.fori_loop(2, 4, mix_back, 0)
-    batch2.first_to_second()
-    batch2.third.first_to_second()
-    few.to_y()
+    batch2.z_to_gather()
+    batch1.third.y_to_second()
     lax.fori_loop(4, 6, mix_back, 0)
     for l in range(LANES):
         lanes = slice(l * 128, (l + 1) * 128)
@@ -850,27 +853,23 @@
             )
     for copy in direct:
         copy.start()
-    batch1.third.y_to_second()
-    batch1.z_to_gather()
-    batch2.second_to_z()
-    batch2.third.second_to_y()
-    few.to_z()
+    batch1.gather_to_second()
+    few.to_y()
+    batch2.third.y_to_second()
+    batch2.gather_to_second()
     batch1.third.second_to_first()
-    batch1.gather_to_second()
-    batch2.third.y_to_second()
-    batch2.z_to_gather()
     for each in (few, batch1, batch1.third, batch2, batch2.third):
         each.settle()
+    batch1.second_to_first()
+    few.to_z()
+    batch2.third.second_to_first()
+    batch2.second_to_first()
+    batch1.third.first_to_core()
+    batch1.first_to_core()
     few.to_gather()
-    batch1.second_to_first()
-    batch2.third.second_to_first()
-    batch2.gather_to_second()
-    few.to_core()
-    batch1.third.first_to_core()
-    batch2.second_to_first()
-    batch1.first_to_core()
     batch2.third.first_to_core()
     batch2.first_to_core()
+    few.to_core()
     for copy in sum(halo1 + halo2, []) + far_copies + [near_copy] + relays:
         copy.wait_send()
     for copy in direct:
@@ -972,7 +971,7 @@
         vmem((4, 80, D), F32),
         vmem((D, D), F32),
         vmem((D, D), BF16),
-        vmem((D, BLOCK), BF16),
+        vmem((D, FFN), BF16),
         vmem((D, D), F32),
         vmem((LANES, 64, 128), F32),
         pltpu.SemaphoreType.DMA((13,)),

time: 77.9 us -> 74.7 us (0.959)
  Pallas kernels: 77.2 us -> 73.8 us
    pallas_call x1, Pallas kernels: 74.7 us -> 71.3 us  [on_device(): pl.pallas_call(lambda *refs: work(sizes, *refs), out_shape=(*(jax.ShapeDt...]
where the time goes in v4:
time: 74.7 us; the launch traced here: 74.6 us
  Pallas kernels  73.8 us (99%)
  between operations  0.8 us (1%)
    pallas_call x1, Pallas kernels, on_device(): pl.pallas_call(lambda *refs: work(sizes, *refs), out_shape=(*(jax.ShapeDt...  71.3 us
    pallas_call x1, Pallas kernels, on_device(): pl.pallas_call(finish, out_shape=tuple((jax.ShapeDtypeStruct(shape, F32)...  2.5 us

profile of v4, /device:TPU:1, one launch (start us, length us, event | category | flops | bytes accessed | tf_op | source)
XLA Modules:
  0.0 74.6 jit_solution(1082939598941031324)
XLA Ops:
  0.6 71.3 %block_pass.1 = (bf16[2,2048,128]{2,1,0:T(8,128)(2,1)S(1)}, bf16[2,512,128]{2,1,0:T(8,128)(2,1)S(1)}, bf16[2,2048,128]{2,1,0:T(8,128)(2,1)S(1)}, bf16[2,512,128]...) custom-call(bf16[2,12,16,384]{3,2,1,0:T(8,128)(2,1)} %refs_0_.1, ...), custom_call_target="tpu_custom_call" | custom-call | tf_op jit(solution)/shard_map/block_pass/pallas_call | solution.py:988
  72.0 2.5 %finish.1 = (f32[2,12,16,384]{3,2,1,0:T(8,128)}, f32[7,7,384]{2,1,0:T(8,128)}, f32[384]{0:T(512)}, f32[384,1536]{1,0:T(8,128)}, f32[1536,384]{1,0:T(8,128)}, /*index=5*/f32[77,384]{1,0:T(8,128)}) custom-call(bf16[2,2048,128]{2,1,0:T(8,128)(2,1)S(1)} %get-tuple-element.18.o1, bf16[2,512,128]{2,1,0:T(8,128)(2,1)S(1)} %get-tuple-element.19.t1, ...), custom_call_target="tpu_custom_call" | custom-call | tf_op jit(solution)/shard_map/finish/pallas_call | solution.py:1004

commit v5 on v4

--- a/solution.py
+++ b/solution.py
@@ -540,17 +540,14 @@
 
     def clear(i, _):
         l, m = lax.div(i, 2), lax.rem(i, 2)
-        for ref in (ext, dext):
-            ref[l, m, 0:3] = jnp.zeros((3, 32, 128), F32)
-            ref[l, m, 15:18] = jnp.zeros((3, 32, 128), F32)
+        ext[l, m, 0:3] = jnp.zeros((3, 32, 128), F32)
+        ext[l, m, 15:18] = jnp.zeros((3, 32, 128), F32)
         ext[l, m, 3:15, 0:8] = jnp.zeros((12, 8, 128), F32)
         ext[l, m, 3:15, 24:32] = jnp.zeros((12, 8, 128), F32)
         return 0
 
     lax.fori_loop(0, 2 * LANES, clear, 0)
-    gk[...] = jnp.zeros_like(gk)
     rim[...] = jnp.zeros_like(rim)
-    few.g[...] = jnp.zeros_like(few.g)
     for copy in loads:
         copy.wait()
     for l in range(LANES):
@@ -594,23 +591,8 @@
     pl.semaphore_wait(barrier, len(peers))
     halo1 = halo(hs, hr, 0)
 
-    for copy in tap_loads + later:
+    for copy in tap_loads:
         copy.wait()
-    for index in range(32):
-        put_small(batch1.g, index, jnp.zeros((16, 128), F32))
-        if index >= 15:
-            put_small(batch2.g, index, jnp.zeros((16, 128), F32))
-    outputs = head.shape[0]
-    head_t[...] = jnp.concatenate([head[...].astype(F32), jnp.zeros((80 - outputs, D), F32)], axis=0).astype(BF16)
-    diagonal = lax.broadcasted_iota(jnp.int32, (16, 16), 0) == lax.broadcasted_iota(jnp.int32, (16, 16), 1)
-    tall[...] = jnp.zeros_like(tall)
-    for a in range(12):
-        water = jnp.broadcast_to(sea[a : a + 1, :].astype(F32), (16, 16))
-        water = jnp.sum(jnp.where(diagonal, water, 0.0), axis=1, keepdims=True)
-        for at in (a * 16,) if a < 8 else (a * 16, a * 16 + 64):
-            tall[at : at + 16, 0:outputs] = target[a]
-            tall[at : at + 16, outputs : outputs + 1] = water
-    tg[...] = tall[...].T[0:80]
     def correlate(field, l, m, flip):
         total = jnp.zeros((12, 16, 128), F32)
         for j in range(7):
@@ -647,6 +629,10 @@
         unpack(ext, hr, l)
         lax.fori_loop(0, 2, lambda m, _, l=l: (edges(l, m), 0)[1], 0)
 
+    for copy in later:
+        copy.wait()
+    outputs = head.shape[0]
+    head_t[...] = jnp.concatenate([head[...].astype(F32), jnp.zeros((80 - outputs, D), F32)], axis=0).astype(BF16)
     gain_row = gain[...].reshape(1, D)
 
     def norm(i, _):
@@ -664,16 +650,16 @@
             normed[rows, lanes] = (value * gain_row[:, lanes]).astype(BF16)
         return 0
 
-    lax.fori_loop(0, 6, norm, 0)
+    lax.fori_loop(0, 6, norm, 0, unroll=True)
 
     total = xb[...].reshape(D, D).astype(F32)
     for b in range(BLOCKS):
         columns = slice(b * BLOCK, (b + 1) * BLOCK)
-        before[...] = dot(normed[...], we[:, columns], NN)
-
-        def gelu(i, _):
+        before[b] = dot(normed[...], we[:, columns], NN)
+
+        def gelu(i, _, b=b, columns=columns):
             rows = pl.ds(pl.multiple_of(i * 32, 32), 32)
-            v = before[rows, :]
+            v = before[b, rows, :]
             square = v * v
             scale = 0.7978845608028654
             t = jnp.tanh(v * (scale + (scale * 0.044715) * square))
@@ -682,7 +668,7 @@
             slope[rows, columns] = half + (0.5 * v) * (1.0 - t * t) * (scale + (scale * 3 * 0.044715) * square)
             return 0
 
-        lax.fori_loop(0, 12, gelu, 0)
+        lax.fori_loop(0, 12, gelu, 0, unroll=True)
         total = total + dot(hidden[:, columns], wr[columns, :], NN)
     block[...] = total.astype(BF16)
 
@@ -700,6 +686,29 @@
     ]
     for copy in [*far_copies, near_copy]:
         copy.start()
+    for index in range(32):
+        put_small(batch1.g, index, jnp.zeros((16, 128), F32))
+        if index >= 15:
+            put_small(batch2.g, index, jnp.zeros((16, 128), F32))
+    gk[...] = jnp.zeros_like(gk)
+    few.g[...] = jnp.zeros_like(few.g)
+
+    def clear_back(i, _):
+        l, m = lax.div(i, 2), lax.rem(i, 2)
+        dext[l, m, 0:3] = jnp.zeros((3, 32, 128), F32)
+        dext[l, m, 15:18] = jnp.zeros((3, 32, 128), F32)
+        return 0
+
+    lax.fori_loop(0, 2 * LANES, clear_back, 0)
+    diagonal = lax.broadcasted_iota(jnp.int32, (16, 16), 0) == lax.broadcasted_iota(jnp.int32, (16, 16), 1)
+    tall[...] = jnp.zeros_like(tall)
+    for a in range(12):
+        water = jnp.broadcast_to(sea[a : a + 1, :].astype(F32), (16, 16))
+        water = jnp.sum(jnp.where(diagonal, water, 0.0), axis=1, keepdims=True)
+        for at in (a * 16,) if a < 8 else (a * 16, a * 16 + 64):
+            tall[at : at + 16, 0:outputs] = target[a]
+            tall[at : at + 16, outputs : outputs + 1] = water
+    tg[...] = tall[...].T[0:80]
     normed_t[...] = normed[...].T
     for b in range(BLOCKS):
         hidden_t[b * BLOCK : (b + 1) * BLOCK, :] = hidden[:, b * BLOCK : (b + 1) * BLOCK].T
@@ -739,14 +748,14 @@
 
     for b in range(BLOCKS):
         columns = slice(b * BLOCK, (b + 1) * BLOCK)
-        before[...] = dot(d_block_b[...], wr[columns, :], NT)
-
-        def gate(i, _):
+        before[b] = dot(d_block_b[...], wr[columns, :], NT)
+
+        def gate(i, _, b=b, columns=columns):
             rows = pl.ds(pl.multiple_of(i * 32, 32), 32)
-            d_before[rows, columns] = (before[rows, :] * slope[rows, columns]).astype(BF16)
+            d_before[rows, columns] = (before[b, rows, :] * slope[rows, columns]).astype(BF16)
             return 0
 
-        lax.fori_loop(0, 12, gate, 0)
+        lax.fori_loop(0, 12, gate, 0, unroll=True)
         grad_expand = dot(normed_t[...], d_before[:, columns], NN)
         for l in range(BLOCK // 128):
             put_main(batch2, (b * (BLOCK // 128) + l) * D, grad_expand[:, l * 128 : (l + 1) * 128])
@@ -776,7 +785,7 @@
             mixed[l, pl.ds(i * 4, 4)] = (recip[rows, :] * (scaled[l] - mean - std[l] * along)).reshape(4, 16, 128)
         return 0
 
-    lax.fori_loop(0, 6, unnorm, 0)
+    lax.fori_loop(0, 6, unnorm, 0, unroll=True)
     for l in range(LANES):
         for m in range(2):
             dext[l, m, 3:11, 8:24, :] = mixed[l, m * 8 : m * 8 + 8]
@@ -961,7 +970,7 @@
         vmem((D, D), F32),
         vmem((D, 128), F32),
         vmem((D, D), BF16),
-        vmem((D, BLOCK), F32),
+        vmem((BLOCKS, D, BLOCK), F32),
         vmem((D, FFN), F32),
         vmem((D, FFN), BF16),
         vmem((FFN, D), BF16),

time: 74.7 us -> 72.5 us (0.971)
  Pallas kernels: 73.8 us -> 71.6 us
    pallas_call x1, Pallas kernels: 71.3 us -> 69.1 us  [on_device(): pl.pallas_call(lambda *refs: work(sizes, *refs), out_shape=(*(jax.ShapeDt...]
where the time goes in v5:
time: 72.5 us; the launch traced here: 72.4 us
  Pallas kernels  71.6 us (99%)
  between operations  0.8 us (1%)
    pallas_call x1, Pallas kernels, on_device(): pl.pallas_call(lambda *refs: work(sizes, *refs), out_shape=(*(jax.ShapeDt...  69.1 us
    pallas_call x1, Pallas kernels, on_device(): pl.pallas_call(finish, out_shape=tuple((jax.ShapeDtypeStruct(shape, F32)...  2.5 us

profile of v5, /device:TPU:1, one launch (start us, length us, event | category | flops | bytes accessed | tf_op | source)
XLA Modules:
  0.0 72.4 jit_solution(3375876877065454845)
XLA Ops:
  0.6 69.1 %block_pass.1 = (bf16[2,2048,128]{2,1,0:T(8,128)(2,1)S(1)}, bf16[2,512,128]{2,1,0:T(8,128)(2,1)S(1)}, bf16[2,2048,128]{2,1,0:T(8,128)(2,1)S(1)}, bf16[2,512,128]...) custom-call(bf16[2,12,16,384]{3,2,1,0:T(8,128)(2,1)} %refs_0_.1, ...), custom_call_target="tpu_custom_call" | custom-call | tf_op jit(solution)/shard_map/block_pass/pallas_call | solution.py:997
  69.7 2.5 %finish.1 = (f32[2,12,16,384]{3,2,1,0:T(8,128)}, f32[7,7,384]{2,1,0:T(8,128)}, f32[384]{0:T(512)}, f32[384,1536]{1,0:T(8,128)}, f32[1536,384]{1,0:T(8,128)}, /*index=5*/f32[77,384]{1,0:T(8,128)}) custom-call(bf16[2,2048,128]{2,1,0:T(8,128)(2,1)S(1)} %get-tuple-element.18.o1, bf16[2,512,128]{2,1,0:T(8,128)(2,1)S(1)} %get-tuple-element.19.t1, ...), custom_call_target="tpu_custom_call" | custom-call | tf_op jit(solution)/shard_map/finish/pallas_call | solution.py:1013

commit v6 on v5

--- a/solution.py
+++ b/solution.py
@@ -280,9 +280,9 @@
                 self.out_core[h].start(came, came, self.p.other_core())
 
     def finish(self):
+        self.settle()
         for group in self.out_core:
             group.received()
-        self.settle()
 
 
 class Few(Copies):
@@ -343,9 +343,9 @@
             self.last.start(came, came, p.other_core())
 
     def finish(self):
+        self.settle()
+        self.kept.wait()
         self.last.received()
-        self.kept.wait()
-        self.settle()
 
 
 class Third(Copies):
@@ -415,8 +415,8 @@
         self.last = self.one(self.out.at[p.core], self.out.at[p.core], p.other_core())
 
     def finish(self):
+        self.settle()
         self.last.received()
-        self.settle()
 
 
 def third_scratch(sizes):
@@ -530,13 +530,16 @@
         pltpu.make_async_copy(target_hbm, target, in_sems.at[11]),
         pltpu.make_async_copy(sea_hbm, sea, in_sems.at[12]),
     ]
-    for copy in loads + tap_loads + later:
+    for copy in loads:
         copy.start()
 
     barrier = pltpu.get_barrier_semaphore()
     peers = place.everyone()
     for peer in peers:
         pl.semaphore_signal(barrier, inc=1, device_id=peer, device_id_type=pl.DeviceIdType.MESH)
+
+    for copy in tap_loads + later:
+        copy.start()
 
     def clear(i, _):
         l, m = lax.div(i, 2), lax.rem(i, 2)
@@ -835,12 +838,13 @@
         return 0
 
     lax.fori_loop(0, 2, mix_back, 0)
+    few.to_x()
     batch1.z_to_gather()
     batch2.third.second_to_y()
-    few.to_x()
     lax.fori_loop(2, 4, mix_back, 0)
+    batch1.third.y_to_second()
     batch2.z_to_gather()
-    batch1.third.y_to_second()
+    few.to_y()
     lax.fori_loop(4, 6, mix_back, 0)
     for l in range(LANES):
         lanes = slice(l * 128, (l + 1) * 128)
@@ -862,23 +866,20 @@
             )
     for copy in direct:
         copy.start()
+    batch2.third.y_to_second()
     batch1.gather_to_second()
-    few.to_y()
-    batch2.third.y_to_second()
+    few.to_z()
+    batch1.third.second_to_first()
     batch2.gather_to_second()
-    batch1.third.second_to_first()
-    for each in (few, batch1, batch1.third, batch2, batch2.third):
-        each.settle()
+    batch2.third.second_to_first()
     batch1.second_to_first()
-    few.to_z()
-    batch2.third.second_to_first()
+    few.to_gather()
     batch2.second_to_first()
     batch1.third.first_to_core()
+    few.to_core()
     batch1.first_to_core()
-    few.to_gather()
     batch2.third.first_to_core()
     batch2.first_to_core()
-    few.to_core()
     for copy in sum(halo1 + halo2, []) + far_copies + [near_copy] + relays:
         copy.wait_send()
     for copy in direct:

time: 72.5 us -> 71.5 us (0.986)
  Pallas kernels: 71.6 us -> 70.6 us
    pallas_call x1, Pallas kernels: 69.1 us -> 68.1 us  [on_device(): pl.pallas_call(lambda *refs: work(sizes, *refs), out_shape=(*(jax.ShapeDt...]
where the time goes in v6:
time: 71.5 us; the launch traced here: 71.4 us
  Pallas kernels  70.6 us (99%)
  between operations  0.8 us (1%)
    pallas_call x1, Pallas kernels, on_device(): pl.pallas_call(lambda *refs: work(sizes, *refs), out_shape=(*(jax.ShapeDt...  68.1 us
    pallas_call x1, Pallas kernels, on_device(): pl.pallas_call(finish, out_shape=tuple((jax.ShapeDtypeStruct(shape, F32)...  2.5 us

profile of v6, /device:TPU:1, one launch (start us, length us, event | category | flops | bytes accessed | tf_op | source)
XLA Modules:
  0.0 71.4 jit_solution(15819961491757202345)
XLA Ops:
  0.6 68.1 %block_pass.1 = (bf16[2,2048,128]{2,1,0:T(8,128)(2,1)S(1)}, bf16[2,512,128]{2,1,0:T(8,128)(2,1)S(1)}, bf16[2,2048,128]{2,1,0:T(8,128)(2,1)S(1)}, bf16[2,512,128]...) custom-call(bf16[2,12,16,384]{3,2,1,0:T(8,128)(2,1)} %refs_0_.1, ...), custom_call_target="tpu_custom_call" | custom-call | tf_op jit(solution)/shard_map/block_pass/pallas_call | solution.py:998
  68.8 2.5 %finish.1 = (f32[2,12,16,384]{3,2,1,0:T(8,128)}, f32[7,7,384]{2,1,0:T(8,128)}, f32[384]{0:T(512)}, f32[384,1536]{1,0:T(8,128)}, f32[1536,384]{1,0:T(8,128)}, /*index=5*/f32[77,384]{1,0:T(8,128)}) custom-call(bf16[2,2048,128]{2,1,0:T(8,128)(2,1)S(1)} %get-tuple-element.18.o1, bf16[2,512,128]{2,1,0:T(8,128)(2,1)S(1)} %get-tuple-element.19.t1, ...), custom_call_target="tpu_custom_call" | custom-call | tf_op jit(solution)/shard_map/finish/pallas_call | solution.py:1014

commit v7 on v6

--- a/solution.py
+++ b/solution.py
@@ -630,7 +630,7 @@
         for copy in halo1[l]:
             copy.wait_recv()
         unpack(ext, hr, l)
-        lax.fori_loop(0, 2, lambda m, _, l=l: (edges(l, m), 0)[1], 0)
+        lax.fori_loop(0, 2, lambda m, _, l=l: (edges(l, m), 0)[1], 0, unroll=True)
 
     for copy in later:
         copy.wait()

time: 71.5 us -> 71.1 us (level)
  no operation moved by 1% of the time
where the time goes in v7:
time: 71.1 us; the launch traced here: 71 us
  Pallas kernels  70.2 us (99%)
  between operations  0.8 us (1%)
    pallas_call x1, Pallas kernels, on_device(): pl.pallas_call(lambda *refs: work(sizes, *refs), out_shape=(*(jax.ShapeDt...  67.7 us
    pallas_call x1, Pallas kernels, on_device(): pl.pallas_call(finish, out_shape=tuple((jax.ShapeDtypeStruct(shape, F32)...  2.5 us

profile of v7, /device:TPU:1, one launch (start us, length us, event | category | flops | bytes accessed | tf_op | source)
XLA Modules:
  0.0 71.0 jit_solution(11990532940825353172)
XLA Ops:
  0.6 67.7 %block_pass.1 = (bf16[2,2048,128]{2,1,0:T(8,128)(2,1)S(1)}, bf16[2,512,128]{2,1,0:T(8,128)(2,1)S(1)}, bf16[2,2048,128]{2,1,0:T(8,128)(2,1)S(1)}, bf16[2,512,128]...) custom-call(bf16[2,12,16,384]{3,2,1,0:T(8,128)(2,1)} %refs_0_.1, ...), custom_call_target="tpu_custom_call" | custom-call | tf_op jit(solution)/shard_map/block_pass/pallas_call | solution.py:998
  68.3 2.5 %finish.1 = (f32[2,12,16,384]{3,2,1,0:T(8,128)}, f32[7,7,384]{2,1,0:T(8,128)}, f32[384]{0:T(512)}, f32[384,1536]{1,0:T(8,128)}, f32[1536,384]{1,0:T(8,128)}, /*index=5*/f32[77,384]{1,0:T(8,128)}) custom-call(bf16[2,2048,128]{2,1,0:T(8,128)(2,1)S(1)} %get-tuple-element.18.o1, bf16[2,512,128]{2,1,0:T(8,128)(2,1)S(1)} %get-tuple-element.19.t1, ...), custom_call_target="tpu_custom_call" | custom-call | tf_op jit(solution)/shard_map/finish/pallas_call | solution.py:1014
